TPU v7x, 256 devices: a whole 4x4x8 slice. The times are simulated.
256 devices in a mesh: frames: 32 (over z, x), heads: 2 (over core), dp: 4 (over y).
Axes of the slice: x: 4, y: 4, z: 8, core: 2. Of those that a mesh axis runs over, the one named last changes fastest.
Arguments:
- queries: bfloat16 [4, 1536, 4096], P('dp', 'heads', 'frames'), may hold values from -5.5 to 5.5
- keys: bfloat16 [4, 1536, 4096], P('dp', 'heads', 'frames'), may hold values from -5.5 to 5.5
- values: bfloat16 [4, 1536, 4096], P('dp', 'heads', 'frames'), may hold values from -6 to 6
- grad_out: bfloat16 [4, 1536, 4096], P('dp', 'heads', 'frames'), may hold values from -6 to 6
- out_weight: bfloat16 [1536, 1536], P('heads'), may hold values from -0.15625 to 0.15625
- head_mask: int32 [24], P('heads'), may hold values from 0 to 1, as said below
- lengths: int32 [4], P('dp'), may hold values from 1024 to 4096
- conv_input: bfloat16 [4, 1536, 4096], P('dp', 'heads', 'frames'), may hold values from -6 to 6
- conv_grad: bfloat16 [4, 1536, 4096], P('dp', 'heads', 'frames'), may hold values from -6 to 6
- conv_weight: float32 [31, 1536], P(None, 'heads'), may hold values from -1 to 1
Outputs:
- grad_queries: bfloat16 [4, 1536, 4096], P('dp', 'heads', 'frames')
- grad_keys: bfloat16 [4, 1536, 4096], P('dp', 'heads', 'frames')
- grad_values: bfloat16 [4, 1536, 4096], P('dp', 'heads', 'frames')
- grad_out_weight: float32 [1536, 1536], P('heads')
- grad_conv_input: bfloat16 [4, 1536, 4096], P('dp', 'heads', 'frames')
- grad_conv_weight: float32 [31, 1536], P(None, 'heads')
Inputs may be any that keep to these rules, and one draw needn't show every extreme that they name: `head_mask`: exactly 6 heads are pruned.
All inputs are finite; a program needn't handle non-finite values.
Results may differ from a plain program's by a relative error of at most 0.0094.
Values may be sent and summed in bfloat16 or wider, within the bound.
No kernel may reach another device: no remote copies, remote signals or barrier semaphores. Data moves between devices by JAX's collectives and lax.ppermute only.
A program may use at most 192 MiB of HBM per device.

v0:
```python
import math

import jax
import jax.numpy as jnp
from jax import lax
from jax.sharding import PartitionSpec as P

DH = 64
KW = 31


def with_halo(cells, sides, width):
    for axis, dim in sides:
        count = lax.axis_size(axis)
        ends = count - 1
        head = lax.slice_in_dim(cells, 0, width, axis=dim)
        tail = lax.slice_in_dim(cells, cells.shape[dim] - width, cells.shape[dim], axis=dim)
        cells = jnp.concatenate(
            [
                lax.ppermute(tail, axis, [(i, (i + 1) % count) for i in range(ends)]),
                cells,
                lax.ppermute(head, axis, [((i + 1) % count, i) for i in range(ends)]),
            ],
            axis=dim,
        )
    return cells


def masked_scores(query_part, key_part, offset, length):
    scores = (
        jnp.einsum("qhd,khd->hqk", query_part, key_part, preferred_element_type=jnp.float32) * 0.125
    )
    usable = offset + jnp.arange(key_part.shape[0], dtype=jnp.int32) < length
    return (scores, usable)


def weighting(scores, usable, log_rows):
    return jnp.where(usable[None, None, :], jnp.exp(scores - log_rows[..., None]), 0.0)


def key_terms(key_part, value_part, offset, query_part, grad_part, log_rows, delta_rows, length):
    scores, usable = masked_scores(query_part, key_part, offset, length)
    probability = weighting(scores, usable, log_rows)
    grad_prob = jnp.einsum(
        "qhd,khd->hqk", grad_part, value_part, preferred_element_type=jnp.float32
    )
    grad_score = (probability * (grad_prob - delta_rows[..., None])).astype(jnp.bfloat16)
    grad_key = jnp.einsum(
        "hqk,qhd->khd", grad_score, query_part, preferred_element_type=jnp.float32
    )
    grad_value = jnp.einsum(
        "hqk,qhd->khd",
        probability.astype(jnp.bfloat16),
        grad_part,
        preferred_element_type=jnp.float32,
    )
    return (grad_key, grad_value)


def per_device(
    queries,
    keys,
    values,
    grad_out,
    out_weight,
    head_mask,
    lengths,
    conv_input,
    conv_grad,
    conv_weight,
):
    heads_here = out_weight.shape[0] // DH
    frames_here = queries.shape[2]
    width_here = heads_here * DH
    length = lengths[0]
    mask_cols = jnp.repeat(head_mask.astype(jnp.float32), DH)
    query_rows = queries[0].T.reshape(frames_here, heads_here, DH)
    own_keys = keys[0].T.reshape(frames_here, heads_here, DH)
    own_values = values[0].T.reshape(frames_here, heads_here, DH)
    grad_full = lax.all_gather(grad_out[0], "heads", axis=0, tiled=True)
    grad_ctx = jnp.einsum("dt,hd->th", grad_full, out_weight, preferred_element_type=jnp.float32)
    grad_rows = (grad_ctx * mask_cols).astype(jnp.bfloat16).reshape(frames_here, heads_here, DH)
    whole_keys, whole_values = (
        lax.all_gather(own_keys, "frames", axis=0, tiled=True),
        lax.all_gather(own_values, "frames", axis=0, tiled=True),
    )
    total_rows = whole_keys.shape[0]
    block_rows = math.gcd(total_rows, 512)
    block_count = total_rows // block_rows
    key_blocks = whole_keys.reshape(block_count, block_rows, heads_here, DH)
    value_blocks = whole_values.reshape(block_count, block_rows, heads_here, DH)
    block_offsets = jnp.arange(block_count, dtype=jnp.int32) * block_rows
    sweep = (key_blocks, value_blocks, block_offsets)

    def stats_step(running, element):
        highest, weight_sum = running
        key_part, value_part, offset = element
        scores, usable = masked_scores(query_rows, key_part, offset, length)
        block_high = jnp.max(jnp.where(usable[None, None, :], scores, -1e30), axis=2)
        new_high = jnp.maximum(highest, block_high)
        added = jnp.sum(
            jnp.where(usable[None, None, :], jnp.exp(scores - new_high[..., None]), 0.0), axis=2
        )
        return ((new_high, weight_sum * jnp.exp(highest - new_high) + added), None)

    start_high = jnp.full((heads_here, frames_here), -1e30, jnp.float32)
    start_sum = jnp.zeros((heads_here, frames_here), jnp.float32)
    (highest, weight_sum), _ = lax.scan(stats_step, (start_high, start_sum), sweep)
    log_total = highest + jnp.log(weight_sum)

    def context_step(running, element):
        key_part, value_part, offset = element
        scores, usable = masked_scores(query_rows, key_part, offset, length)
        weights = weighting(scores, usable, log_total).astype(jnp.bfloat16)
        return (
            running
            + jnp.einsum("hqk,khd->qhd", weights, value_part, preferred_element_type=jnp.float32),
            None,
        )

    zero_rows = jnp.zeros((frames_here, heads_here, DH), jnp.float32)
    context, _ = lax.scan(context_step, zero_rows, sweep)
    row_delta = jnp.sum(grad_rows.astype(jnp.float32) * context, axis=2).T

    def query_step(running, element):
        key_part, value_part, offset = element
        scores, usable = masked_scores(query_rows, key_part, offset, length)
        probability = weighting(scores, usable, log_total)
        grad_prob = jnp.einsum(
            "qhd,khd->hqk", grad_rows, value_part, preferred_element_type=jnp.float32
        )
        grad_score = (probability * (grad_prob - row_delta[..., None])).astype(jnp.bfloat16)
        return (
            running
            + jnp.einsum("hqk,khd->qhd", grad_score, key_part, preferred_element_type=jnp.float32),
            None,
        )

    grad_query_sum, _ = lax.scan(query_step, zero_rows, sweep)
    grad_queries = (
        (grad_query_sum * 0.125).astype(jnp.bfloat16).reshape(frames_here, width_here).T[None]
    )
    piece_rows = math.gcd(lax.axis_size("frames") * frames_here, 512)
    pieces = lax.axis_size("frames") * frames_here // piece_rows
    key_part = whole_keys.reshape(pieces, piece_rows, heads_here, DH)
    value_part = whole_values.reshape(pieces, piece_rows, heads_here, DH)
    piece_offsets = jnp.arange(pieces, dtype=jnp.int32) * piece_rows

    def per_piece(element):
        grad_key, grad_value = key_terms(
            element[0], element[1], element[2], query_rows, grad_rows, log_total, row_delta, length
        )
        return jnp.concatenate(
            [grad_key.reshape(piece_rows, width_here), grad_value.reshape(piece_rows, width_here)],
            axis=1,
        )

    summed = lax.psum_scatter(
        lax.map(per_piece, (key_part, value_part, piece_offsets)).reshape(
            lax.axis_size("frames") * frames_here, 2 * width_here
        ),
        "frames",
        scatter_dimension=0,
        tiled=True,
    )
    key_sum = summed[:, :width_here]
    value_sum = summed[:, width_here:]
    grad_keys = (key_sum * 0.125).astype(jnp.bfloat16).T[None]
    grad_values = value_sum.astype(jnp.bfloat16).T[None]
    context_masked = (context.reshape(frames_here, width_here) * mask_cols).astype(jnp.bfloat16)
    out_part = jnp.einsum(
        "th,dt->hd", context_masked, grad_full, preferred_element_type=jnp.float32
    )
    half_width = KW // 2
    stacked = jnp.stack([conv_input[0], conv_grad[0]])
    rimmed = with_halo(stacked, (("frames", 2),), half_width)
    input_wide = rimmed[0].astype(jnp.float32)
    grad_wide = rimmed[1].astype(jnp.float32)
    own_grad = conv_grad[0].astype(jnp.float32)
    grad_input = jnp.zeros(own_grad.shape, jnp.float32)
    tap_sums = []
    for tap_index in range(KW):
        begin = 2 * half_width - tap_index
        grad_input = (
            grad_input + conv_weight[tap_index][:, None] * grad_wide[:, begin : begin + frames_here]
        )
        tap_sums.append(
            jnp.sum(own_grad * input_wide[:, tap_index : tap_index + frames_here], axis=1)
        )
    conv_part = jnp.stack(tap_sums)
    out_total, conv_total = lax.psum((out_part, conv_part), ("frames", "dp"))
    return (
        grad_queries,
        grad_keys,
        grad_values,
        out_total,
        grad_input.astype(jnp.bfloat16)[None],
        conv_total,
    )


def solution(mesh):
    placed = (
        P("dp", "heads", "frames"),
        P("dp", "heads", "frames"),
        P("dp", "heads", "frames"),
        P("dp", "heads", "frames"),
        P("heads", None),
        P("heads"),
        P("dp"),
        P("dp", "heads", "frames"),
        P("dp", "heads", "frames"),
        P(None, "heads"),
    )
    return jax.shard_map(
        per_device,
        mesh=mesh,
        in_specs=placed,
        out_specs=(
            P("dp", "heads", "frames"),
            P("dp", "heads", "frames"),
            P("dp", "heads", "frames"),
            P("heads", None),
            P("dp", "heads", "frames"),
            P(None, "heads"),
        ),
        check_vma=False,
    )
```

profile of v0, /device:TPU:4, one launch (start us, length us, event | category | flops | bytes accessed | tf_op | source)
XLA Modules:
  0.0 1447.1 jit_solution(15280238868027512041)
XLA Ops:
  14.3 92.0 %all-gather.4.cloned.1.call-done = bf16[4096,12,64]{0,2,1:T(8,128)(2,1)} async-done(((bf16[128,12,64]{0,2,1:T(8,128)(2,1)}), bf16[4096,12,64]{0,2,1:T(8,128)(2,1)}) %all-gather.4.cloned.1.call-update) | async-done | bytes 6291472 | tf_op jit(solution)/shard_map/all_gather | solution.py:84
  106.3 6.4 copy.88
  112.6 54.8 %while.46 = (s32[]{:T(128)}, f32[12,128]{1,0:T(8,128)S(1)}, f32[12,128]{1,0:T(8,128)}, s32[8]{0:T(128)}, s32[]{:T(128)}, /*index=5*/bf16[8,512,12,64]{1,3,2,0:T(...) while((s32[]{:T(128)}, f32[12,128]{1,0:T(8,128)S(1)}, f32[12,128]{1,0:T(8,128)}, ...), condition=%wide.region_3.4_spmd.clone, body=%wide.region_0.3_spmd.clone.sunk | while | flops 106177024 | bytes 7407324 | solution.py:108
  167.4 33.0 %all-gather.6.cloned.1.call-done = bf16[4096,12,64]{0,2,1:T(8,128)(2,1)} async-done(((bf16[128,12,64]{0,2,1:T(8,128)(2,1)}), bf16[4096,12,64]{0,2,1:T(8,128)(2,1)}) %all-gather.6.cloned.1.call-update) | async-done | bytes 6291472 | tf_op jit(solution)/shard_map/all_gather | solution.py:85
  200.4 6.4 copy.87
  206.8 40.9 %while.47 = (s32[]{:T(128)}, f32[128,12,64]{0,2,1:T(8,128)S(1)}, bf16[8,512,12,64]{1,3,2,0:T(8,128)(2,1)}, s32[8]{0:T(128)}, s32[]{:T(128)}, /*index=5*/bf16[8,5...) while((s32[]{:T(128)}, f32[128,12,64]{0,2,1:T(8,128)S(1)}, ...), condition=%wide.region_5.6_spmd.clone, body=%wide.region_4.5_spmd.clone.sunk | while | flops 204669952 | bytes 2564746 | solution.py:122
  248.5 648.0 %while.45 = (s32[]{:T(128)}, f32[8,512,1536]{1,0,2:T(8,128)}, s32[8]{0:T(128)}, s32[]{:T(128)}, bf16[8,512,12,64]{1,3,2,0:T(8,128)(2,1)}, /*index=5*/bf16[128,12...) while((s32[]{:T(128)}, f32[8,512,1536]{1,0,2:T(8,128)}, ...), condition=%wide.region_10.11_spmd, body=%wide.region_9.10_spmd.sunk | while | flops 411304960 | bytes 33838748 | solution.py:159
  254.7 3.9 fusion.172
  260.8 6.0 copy.90
  266.8 62.6 %dynamic_update_slice.5 = f32[8,512,1536]{1,0,2:T(8,128)} dynamic-update-slice(f32[8,512,1536]{1,0,2:T(8,128)} %get-tuple-element.838, f32[1,512,1536]{1,0,2:T(1,128)S(1)} %copy.90, s32[]{:T(128)S(6)} %copy.115, s32[]{:T(128)} %constant.59.clone.1..sunk, s32[]{:T(128)} %constant.59.clone.1..sunk) | dynamic-update-slice | bytes 6291460 | tf_op jit(solution)/shard_map/while/body/jit(dynamic_update_index_in_dim)/dynamic_update_slice | solution.py:159
  335.7 3.9 fusion.172
  341.8 6.0 copy.90
  347.8 62.6 %dynamic_update_slice.5 = f32[8,512,1536]{1,0,2:T(8,128)} dynamic-update-slice(f32[8,512,1536]{1,0,2:T(8,128)} %get-tuple-element.838, f32[1,512,1536]{1,0,2:T(1,128)S(1)} %copy.90, s32[]{:T(128)S(6)} %copy.115, s32[]{:T(128)} %constant.59.clone.1..sunk, s32[]{:T(128)} %constant.59.clone.1..sunk) | dynamic-update-slice | bytes 6291460 | tf_op jit(solution)/shard_map/while/body/jit(dynamic_update_index_in_dim)/dynamic_update_slice | solution.py:159
  416.7 3.9 fusion.172
  422.8 6.0 copy.90
  428.8 62.6 %dynamic_update_slice.5 = f32[8,512,1536]{1,0,2:T(8,128)} dynamic-update-slice(f32[8,512,1536]{1,0,2:T(8,128)} %get-tuple-element.838, f32[1,512,1536]{1,0,2:T(1,128)S(1)} %copy.90, s32[]{:T(128)S(6)} %copy.115, s32[]{:T(128)} %constant.59.clone.1..sunk, s32[]{:T(128)} %constant.59.clone.1..sunk) | dynamic-update-slice | bytes 6291460 | tf_op jit(solution)/shard_map/while/body/jit(dynamic_update_index_in_dim)/dynamic_update_slice | solution.py:159
  497.7 3.9 fusion.172
  503.8 6.0 copy.90
  509.8 62.6 %dynamic_update_slice.5 = f32[8,512,1536]{1,0,2:T(8,128)} dynamic-update-slice(f32[8,512,1536]{1,0,2:T(8,128)} %get-tuple-element.838, f32[1,512,1536]{1,0,2:T(1,128)S(1)} %copy.90, s32[]{:T(128)S(6)} %copy.115, s32[]{:T(128)} %constant.59.clone.1..sunk, s32[]{:T(128)} %constant.59.clone.1..sunk) | dynamic-update-slice | bytes 6291460 | tf_op jit(solution)/shard_map/while/body/jit(dynamic_update_index_in_dim)/dynamic_update_slice | solution.py:159
  578.7 3.9 fusion.172
  584.8 6.0 copy.90
  590.8 62.6 %dynamic_update_slice.5 = f32[8,512,1536]{1,0,2:T(8,128)} dynamic-update-slice(f32[8,512,1536]{1,0,2:T(8,128)} %get-tuple-element.838, f32[1,512,1536]{1,0,2:T(1,128)S(1)} %copy.90, s32[]{:T(128)S(6)} %copy.115, s32[]{:T(128)} %constant.59.clone.1..sunk, s32[]{:T(128)} %constant.59.clone.1..sunk) | dynamic-update-slice | bytes 6291460 | tf_op jit(solution)/shard_map/while/body/jit(dynamic_update_index_in_dim)/dynamic_update_slice | solution.py:159
  659.7 3.9 fusion.172
  665.8 6.0 copy.90
  671.8 62.6 %dynamic_update_slice.5 = f32[8,512,1536]{1,0,2:T(8,128)} dynamic-update-slice(f32[8,512,1536]{1,0,2:T(8,128)} %get-tuple-element.838, f32[1,512,1536]{1,0,2:T(1,128)S(1)} %copy.90, s32[]{:T(128)S(6)} %copy.115, s32[]{:T(128)} %constant.59.clone.1..sunk, s32[]{:T(128)} %constant.59.clone.1..sunk) | dynamic-update-slice | bytes 6291460 | tf_op jit(solution)/shard_map/while/body/jit(dynamic_update_index_in_dim)/dynamic_update_slice | solution.py:159
  740.7 3.9 fusion.172
  746.8 6.0 copy.90
  752.8 62.6 %dynamic_update_slice.5 = f32[8,512,1536]{1,0,2:T(8,128)} dynamic-update-slice(f32[8,512,1536]{1,0,2:T(8,128)} %get-tuple-element.838, f32[1,512,1536]{1,0,2:T(1,128)S(1)} %copy.90, s32[]{:T(128)S(6)} %copy.115, s32[]{:T(128)} %constant.59.clone.1..sunk, s32[]{:T(128)} %constant.59.clone.1..sunk) | dynamic-update-slice | bytes 6291460 | tf_op jit(solution)/shard_map/while/body/jit(dynamic_update_index_in_dim)/dynamic_update_slice | solution.py:159
  821.7 3.9 fusion.172
  827.8 6.0 copy.90
  833.8 62.6 %dynamic_update_slice.5 = f32[8,512,1536]{1,0,2:T(8,128)} dynamic-update-slice(f32[8,512,1536]{1,0,2:T(8,128)} %get-tuple-element.838, f32[1,512,1536]{1,0,2:T(1,128)S(1)} %copy.90, s32[]{:T(128)S(6)} %copy.115, s32[]{:T(128)} %constant.59.clone.1..sunk, s32[]{:T(128)} %constant.59.clone.1..sunk) | dynamic-update-slice | bytes 6291460 | tf_op jit(solution)/shard_map/while/body/jit(dynamic_update_index_in_dim)/dynamic_update_slice | solution.py:159
  896.5 29.5 %copy.84 = f32[192,8,8,512]{3,1,2,0:T(8,128)} copy(f32[192,8,8,512]{3,2,1,0:T(8,128)} %bitcast.206) | data formatting | bytes 50331648
  929.7 3.5 collective-permute-start
  936.9 5.8 collective-permute-done
  946.1 3.7 fusion.88
  952.7 7.5 fusion.129
  964.0 68.6 %while.48 = (s32[]{:T(128)}, f32[128,12,64]{0,2,1:T(8,128)}, bf16[8,512,12,64]{1,3,2,0:T(8,128)(2,1)}, s32[8]{0:T(128)}, s32[]{:T(128)}, /*index=5*/bf16[128,12,...) while((s32[]{:T(128)}, f32[128,12,64]{0,2,1:T(8,128)}, ...), condition=%wide.region_8.9_spmd.clone, body=%wide.region_7.8_spmd.clone.sunk | while | flops 306906112 | bytes 9845406 | solution.py:139
  968.8 3.7 fusion.185
  977.3 3.8 fusion.185
  985.9 3.8 fusion.185
  994.5 3.8 fusion.185
  1003.1 3.8 fusion.185
  1011.7 3.8 fusion.185
  1020.3 3.8 fusion.185
  1028.9 3.8 fusion.185
  1034.4 158.5 %reduce-scatter.2.cloned.1.call-done = f32[128,1536]{0,1:T(8,128)} async-done(((f32[4096,1536]{0,1:T(8,128)}), f32[128,1536]{0,1:T(8,128)}) %reduce-scatter.2.cloned.1.call-update) | async-done | bytes 786448 | tf_op jit(solution)/shard_map/reduce_scatter | solution.py:158
  1196.2 238.7 %all-reduce.3.cloned.1.call-done = (f32[768,1536]{1,0:T(8,128)}, f32[31,768]{1,0:T(8,128)}) async-done(((f32[768,1536]{1,0:T(8,128)}, f32[31,768]{1,0:T(8,128)}), (f32[768,1536]{1,0:T(8,128)}, f32[31,768]{1,0:T(8,128)})) %all-reduce.3.cloned.1.call-update) | async-done | bytes 4813840 | tf_op jit(solution)/shard_map/psum | solution.py:191
  1435.0 5.0 copy.122
  (294 shorter events, 231.5 us)
Async XLA Ops:
  7.2 5.4 copy-start
  7.2 99.1 %all-gather.4.cloned.1.call-start = ((), (), s32[]{:S(2)}) async-start(), calls=%async_computation.1 | async-start | bytes 6488064 | tf_op jit(solution)/shard_map/all_gather | solution.py:84
  7.9 192.5 %all-gather.6.cloned.1.call-start = ((), (), s32[]{:S(2)}) async-start(), calls=%async_computation.2 | async-start | bytes 6488064 | tf_op jit(solution)/shard_map/all_gather | solution.py:85
  8.7 1184.2 %reduce-scatter.2.cloned.1.call-start = ((), (), s32[]{:S(2)}) async-start(), calls=%async_computation.3 | async-start | bytes 25952256 | tf_op jit(solution)/shard_map/reduce_scatter | solution.py:158
  9.6 103.1 %copy-start.16 = (f32[768]{0:T(1024)}, f32[768]{0:T(1024)S(1)}, u32[]{:S(2)}) copy-start(f32[768]{0:T(1024)S(1)} %mul.470) | copy-start | bytes 9220
  11.8 0.8 copy-start.3
  106.3 6.4 copy-start.2
  115.1 0.5 copy-start.15
  117.6 1.3 copy-start.9
  118.9 0.6 copy-start.10
  121.9 0.5 copy-start.15
  124.4 1.3 copy-start.9
  125.7 0.6 copy-start.10
  128.8 0.5 copy-start.15
  131.3 1.3 copy-start.9
  132.6 0.6 copy-start.10
  135.6 0.5 copy-start.15
  138.1 1.3 copy-start.9
  139.4 0.6 copy-start.10
  142.5 0.5 copy-start.15
  145.0 1.3 copy-start.9
  146.3 0.6 copy-start.10
  149.3 0.5 copy-start.15
  151.8 1.3 copy-start.9
  153.1 0.6 copy-start.10
  156.1 0.5 copy-start.15
  158.7 1.3 copy-start.9
  160.0 0.6 copy-start.10
  163.0 0.5 copy-start.15
  165.5 1.3 copy-start.9
  166.8 0.6 copy-start.10
  200.4 6.4 copy-start.11
  200.4 6.4 copy-start.6
  247.7 0.8 copy-start.7
  926.0 0.9 copy-start.12
  926.0 1.0 copy-start.5
  926.0 7.3 copy-start.14
  926.0 509.0 %all-reduce.3.cloned.1.call-start = ((), (), s32[]{:S(2)}) async-start(), calls=%async_computation.4 | async-start | bytes 9633792 | tf_op jit(solution)/shard_map/psum | solution.py:191
  927.2 9.7 collective-permute-start.1
  929.7 13.0 collective-permute-start
  952.6 7.5 copy-start.8
  952.6 7.7 copy-start.4
  952.6 7.7 copy-start.17
  963.3 0.7 copy-start.18
  1435.0 5.7 copy-start.1
  1435.0 5.0 copy-start.13
Sparse Core Ops, SparseCore 0:
  10.5 95.7 all-gather.3
  108.7 91.6 all-gather.5
  926.1 266.6 reduce-scatter.1
  1198.9 236.0 all-reduce.2
where the time goes:
time: 1460 us; the launch traced here: 1450 us
  local copies, waits for them, and re-layouts  653 us (45%)
  waiting for transfers between devices  533 us (37%)
  matrix products  146 us (10%)
  other arithmetic  92.3 us (6%)
    dynamic_update_slice x16, local copies, waits for them, and re-layouts, per_device(): lax.map(per_piece, (key_part, value_part, piece_offsets))  550 us
    psum x1, waiting for transfers between devices, per_device(): out_total, conv_total = lax.psum((out_part, conv_part), ('frames', 'dp'))  239 us
    reduce_scatter x1, waiting for transfers between devices, per_device(): lax.psum_scatter(lax.map(per_piece, (key_part, value_part, piece_offsets)...  158 us
    all_gather x1, waiting for transfers between devices, per_device(): lax.all_gather(own_keys, 'frames', axis=0, tiled=True)  92 us
    lt x32, other arithmetic, masked_scores(): usable = offset + jnp.arange(key_part.shape[0], dtype=jnp.int32) < length  44.9 us
    dot_general x24, matrix products, masked_scores(): jnp.einsum('qhd,khd->hqk', query_part, key_part, preferred_element_type=j...  44.5 us
    dynamic_slice x32, local copies, waits for them, and re-layouts, per_device(): lax.scan(stats_step, (start_high, start_sum), sweep)  38.8 us
    unnamed x36, local copies, waits for them, and re-layouts  37.6 us
  transfers between devices with their start and end apart: 6, of which 6 were waited for; matrix products, arithmetic and copies ran while one was open for 10% of the time, Pallas kernels for 0%

commit v1 on v0

v1 whole, which is shorter than its diff:
```python
import functools
import math

import jax
import jax.numpy as jnp
from jax import lax
from jax.experimental import pallas as pl
from jax.experimental.pallas import tpu as pltpu
from jax.sharding import Mesh, PartitionSpec as P

DH = 64
KW = 31
BF = jnp.bfloat16
F32 = jnp.float32
TWO_SCALE = math.log2(math.e) / 8
QB = 512
KC = 512


def nt(a, b):
    return lax.dot_general(a, b, (((1,), (1,)), ((), ())), preferred_element_type=F32)


def nn(a, b):
    return jnp.dot(a, b, preferred_element_type=F32)


def attention_kernel(
    where_ref, mine, other, mine_q, other_q, xch, ctx_out,
    kt, vt, kn, vn, weights, grad_k, grad_v,
):
    blocks, frames = mine.shape[0], mine.shape[2]
    total = blocks * frames
    step = pl.program_id(0)
    length, core = where_ref[0], where_ref[1]
    chunks = total // KC
    per_chunk = KC // frames

    @pl.when(step == 0)
    def _():
        row = lax.broadcasted_iota(jnp.int32, (frames, DH), 0)
        lane = lax.broadcasted_iota(jnp.int32, (frames, DH), 1)
        ones = jnp.where(lane < 3, 1.0, 0.0).astype(BF)
        for s in range(blocks):
            both = jnp.where(core == 0, mine[s], other[s])
            here = pl.ds(s * frames, frames)
            kn[:, here] = both[:DH]
            vn[:DH, here] = both[DH:]
            turned = both.astype(F32)
            kt[here, :DH] = turned[:DH].T.astype(BF)
            vt[here, :DH] = turned[DH:].T.astype(BF)
            first = ((s % 8) * 4 + s // 8) * frames
            masked = jnp.logical_and(lane == 0, row + first >= length)
            kt[here, DH:] = jnp.where(masked, -1e30, 0.0).astype(BF)
            vt[here, DH:] = ones
        vn[DH:, :] = jnp.ones((vn.shape[0] - DH, total), BF)
        grad_k[...] = jnp.zeros_like(grad_k)
        grad_v[...] = jnp.zeros_like(grad_v)

    sources = QB // frames
    q_parts = [jnp.where(core == 1, mine_q[u], other_q[u]) for u in range(sources)]
    q = jnp.concatenate([p[:DH] for p in q_parts], axis=1)
    g = jnp.concatenate([p[DH:] for p in q_parts], axis=1).astype(F32)
    extra = lax.broadcasted_iota(jnp.int32, (DH, QB), 0)
    q_wide = jnp.concatenate([q, jnp.where(extra == 0, 1.0, 0.0).astype(BF)], axis=0)

    high = jnp.full((1, QB), -1e30, F32)
    highs = []
    sums = jnp.zeros((vn.shape[0], QB), F32)
    for i in range(chunks):
        here = pl.ds(i * KC, KC)
        scores = nn(kt[here, :], q_wide)
        new_high = jnp.maximum(high, jnp.max(scores, axis=0, keepdims=True))
        part = jnp.exp2(scores * TWO_SCALE - new_high * TWO_SCALE).astype(BF)
        weights[here, :] = part
        sums = sums * jnp.exp2((high - new_high) * TWO_SCALE) + nn(vn[:, here], part)
        high = new_high
        highs.append(high)
    inverse = 1.0 / sums[DH : DH + 1]
    context = sums[:DH] * inverse
    grad_q = jnp.zeros((DH, QB), F32)
    for i in range(chunks):
        here = pl.ds(i * KC, KC)
        g_part = (g * (inverse * jnp.exp2((highs[i] - high) * TWO_SCALE))).astype(BF)
        delta = jnp.sum(g_part.astype(F32) * context, axis=0, keepdims=True)
        d0 = delta.astype(BF).astype(F32)
        d1 = (delta - d0).astype(BF).astype(F32)
        d2 = delta - d0 - d1
        rows = jnp.where(
            extra == 0, -d0, jnp.where(extra == 1, -d1, jnp.where(extra == 2, -d2, 0.0))
        )
        g_wide = jnp.concatenate([g_part, rows.astype(BF)], axis=0)
        part = weights[here, :]
        grad_score = (part.astype(F32) * nn(vt[here, :], g_wide)).astype(BF)
        grad_q = grad_q + nn(kn[:, here], grad_score)
        grad_k[here, :] += nt(grad_score, q)
        grad_v[here, :] += nt(part, g_part)
    grad_q = (grad_q * 0.125).astype(BF)
    context = context.astype(BF)
    half = DH // 2
    for u in range(sources):
        cols = slice(u * frames, (u + 1) * frames)
        ctx_out[u] = context[:, cols]
        at = pl.ds(pl.multiple_of(blocks * DH + (step * sources + u) * half, half), half)
        xch[0, at, :] = grad_q[:half, cols]
        xch[1, at, :] = grad_q[half:, cols]

    @pl.when(step == pl.num_programs(0) - 1)
    def _():
        for s in range(blocks):
            here = pl.ds(s * frames, frames)
            to = pl.ds(s * DH, DH)
            xch[0, to, :] = (grad_k[here, :].T * 0.125).astype(BF)
            xch[1, to, :] = grad_v[here, :].T.astype(BF)


def attention(where, mine, other):
    blocks, rows, frames = mine.shape
    total = blocks * frames
    sources = QB // frames
    steps = total // 2 // QB
    flops = 6 * 2 * total * (total // 2) * DH
    whole = pl.BlockSpec((blocks, rows, frames), lambda i, w: (0, 0, 0))
    part = pl.BlockSpec((sources, rows, frames), lambda i, w: (w[1] * steps + i, 0, 0))
    return pl.pallas_call(
        attention_kernel,
        grid_spec=pltpu.PrefetchScalarGridSpec(
            num_scalar_prefetch=1,
            grid=(steps,),
            in_specs=[whole, whole, part, part],
            out_specs=[
                pl.BlockSpec((2, blocks * DH + blocks // 2 * (DH // 2), frames), lambda i, w: (0, 0, 0)),
                pl.BlockSpec((sources, DH, frames), lambda i, w: (i, 0, 0)),
            ],
            scratch_shapes=[
                pltpu.VMEM((total, 2 * DH), BF),
                pltpu.VMEM((total, 2 * DH), BF),
                pltpu.VMEM((DH, total), BF),
                pltpu.VMEM((DH + 16, total), BF),
                pltpu.VMEM((total, QB), BF),
                pltpu.VMEM((total, DH), F32),
                pltpu.VMEM((total, DH), F32),
            ],
        ),
        out_shape=[
            jax.ShapeDtypeStruct((2, blocks * DH + blocks // 2 * (DH // 2), frames), BF),
            jax.ShapeDtypeStruct((blocks // 2, DH, frames), BF),
        ],
        compiler_params=pltpu.CompilerParams(
            dimension_semantics=("arbitrary",), vmem_limit_bytes=48 * 1024 * 1024
        ),
        cost_estimate=pl.CostEstimate(flops=flops, bytes_accessed=4 << 20, transcendentals=total * total // 2),
        name="attention",
    )(where, mine, other, mine, other)


def out_weight_kernel(ctx, grad, out):
    @pl.when(pl.program_id(0) == 0)
    def _():
        out[...] = jnp.zeros_like(out)

    for u in range(ctx.shape[0]):
        out[...] += nt(ctx[u], grad[u])


def out_weight_part(ctx, grad):
    blocks, channels, frames = grad.shape
    each = 4
    return pl.pallas_call(
        out_weight_kernel,
        grid=(blocks // each,),
        in_specs=[
            pl.BlockSpec((each, DH, frames), lambda i: (i, 0, 0)),
            pl.BlockSpec((each, channels, frames), lambda i: (i, 0, 0)),
        ],
        out_specs=pl.BlockSpec((DH, channels), lambda i: (0, 0)),
        out_shape=jax.ShapeDtypeStruct((DH, channels), F32),
        compiler_params=pltpu.CompilerParams(dimension_semantics=("arbitrary",)),
        cost_estimate=pl.CostEstimate(
            flops=2 * blocks * DH * channels * frames, bytes_accessed=7 << 20, transcendentals=0
        ),
        name="out_weight",
    )(ctx, grad)


def with_halo(cells, width):
    frames = cells.shape[2]
    order = [(z, x) for z in range(8) for x in range(4)]
    axes = ("z", "x")
    count = len(order)
    head, tail = cells[:, :, :width], cells[:, :, frames - width :]
    left = lax.ppermute(tail, axes, [(i, i + 1) for i in range(count - 1)])
    right = lax.ppermute(head, axes, [(i + 1, i) for i in range(count - 1)])
    return jnp.concatenate([left, cells, right], axis=2)


def convolution(conv_input, conv_grad, conv_weight):
    frames = conv_grad.shape[1]
    half_width = KW // 2
    rimmed = with_halo(jnp.stack([conv_input, conv_grad]), half_width)
    input_wide = rimmed[0].astype(F32)
    grad_wide = rimmed[1].astype(F32)
    own_grad = conv_grad.astype(F32)
    grad_input = jnp.zeros(own_grad.shape, F32)
    tap_sums = []
    for tap in range(KW):
        begin = 2 * half_width - tap
        grad_input = grad_input + conv_weight[tap][:, None] * grad_wide[:, begin : begin + frames]
        tap_sums.append(jnp.sum(own_grad * input_wide[:, tap : tap + frames], axis=1))
    return grad_input.astype(BF), jnp.stack(tap_sums)


def swap(array):
    return lax.ppermute(array, "c", [(0, 1), (1, 0)])


def to_all(array, axes):
    count = lax.axis_size(axes)
    copies = jnp.broadcast_to(array[None], (count, *array.shape))
    return lax.all_to_all(copies, axes, 0, 0, tiled=True)


def per_device(
    queries, keys, values, grad_out, out_weight, head_mask, lengths, conv_input, conv_grad, conv_weight
):
    heads = out_weight.shape[0] // DH
    frames = queries.shape[2]
    width = heads * DH
    core = lax.axis_index("c")
    wide = ("x", "z")
    blocks = lax.axis_size(wide)

    grad_frames = lax.all_gather(grad_out[0], wide, axis=0, tiled=False)
    grad_full = lax.all_gather(grad_out[0], "c", axis=0, tiled=True)
    mask = jnp.repeat(head_mask.astype(F32), DH)[:, None]
    grad_ctx = (nn(out_weight, grad_full) * mask).astype(BF)

    def by_head(a):
        return a.reshape(heads, DH, frames)

    first = jnp.stack(
        [
            jnp.concatenate([by_head(keys[0]), by_head(values[0])], axis=1),
            jnp.concatenate([by_head(queries[0]), by_head(grad_ctx)], axis=1),
        ]
    )
    by_core = lax.all_to_all(first, "c", 0, 0, tiled=True).reshape(2 * heads, 2 * DH, frames)
    padded = jnp.pad(by_core, ((0, blocks - 2 * heads), (0, 0), (0, 0)))
    mine = lax.all_to_all(padded, wide, 0, 0, tiled=True)
    other = swap(mine)

    where = jnp.stack([lengths[0], core.astype(jnp.int32)])
    xch, ctx = attention(where, mine, other)

    xch = lax.all_to_all(xch, "c", 0, 0, tiled=True)
    key_rows = blocks * DH
    summed = (xch[0, :key_rows].astype(F32) + xch[1, :key_rows].astype(F32)).astype(BF)
    back = jnp.concatenate(
        [
            summed.reshape(blocks, DH, frames),
            xch[:, key_rows:].reshape(blocks, DH // 2, frames),
        ],
        axis=1,
    )
    back = lax.all_to_all(back, wide, 0, 0, tiled=True)[: 2 * heads]
    back = lax.all_to_all(
        back.reshape(2, heads, DH + DH // 2, frames), "c", 0, 0, tiled=True
    )
    grad_keys = back[0, :, :DH].reshape(1, width, frames)
    grad_values = back[1, :, :DH].reshape(1, width, frames)
    grad_queries = jnp.concatenate([back[0, :, DH:], back[1, :, DH:]], axis=1).reshape(
        1, width, frames
    )

    ctx_other = swap(ctx)
    ctx_all = jnp.where(
        core == 0, jnp.concatenate([ctx, ctx_other]), jnp.concatenate([ctx_other, ctx])
    )
    part = out_weight_part(ctx_all, grad_frames).astype(BF)
    cols = width // 2
    pieces = part.reshape(8, 8, 2, cols).transpose(0, 2, 1, 3).reshape(16, 8, cols)
    pieces = lax.all_to_all(pieces, ("x", "y"), 0, 0, tiled=True).reshape(4, 4, 8, cols)
    held = jnp.sum(pieces[:3].astype(F32), axis=1).astype(BF)
    held = to_all(held, "z").transpose(1, 0, 2, 3).reshape(2, heads, 8, cols)
    held = lax.all_to_all(held, "c", 0, 0, tiled=True)
    held = to_all(held, ("x", "y")).reshape(8, 2, 2, heads, 8, cols)
    own_mask = head_mask.astype(F32)[:, None, None, None, None, None]
    grad_out_weight = (held.transpose(3, 0, 4, 2, 1, 5).astype(F32) * own_mask).reshape(width, 2 * width)

    grad_conv_input, conv_part = convolution(conv_input[0], conv_grad[0], conv_weight)
    conv_total = lax.psum(conv_part, ("z", "x", "y"))
    return (
        grad_queries,
        grad_keys,
        grad_values,
        grad_out_weight,
        grad_conv_input[None],
        conv_total,
    )


def solution(mesh):
    fine = Mesh(mesh.devices.reshape(8, 4, 2, 4), ("z", "x", "c", "y"))
    frames = ("z", "x")
    cells = P("y", "c", frames)
    return jax.shard_map(
        per_device,
        mesh=fine,
        in_specs=(
            cells, cells, cells, cells, P("c", None), P("c"), P("y"), cells, cells, P(None, "c"),
        ),
        out_specs=(cells, cells, cells, P("c", None), cells, P(None, "c")),
        check_vma=False,
    )
```

time: 1460 us -> 464 us (0.32)
  local copies, waits for them, and re-layouts: 653 us -> 27.7 us
  waiting for transfers between devices: 533 us -> 252 us
  matrix products: 146 us -> 0.78 us
  other arithmetic: 92.3 us -> 24.4 us
  blocking collectives: 2.29 us -> 54.1 us
  Pallas kernels: 0 us -> 46.3 us
  starting transfers between devices: 6.18 us -> 41.2 us
    dynamic_update_slice x16 -> x0, local copies, waits for them, and re-layouts: 550 us -> none  [per_device(): lax.map(per_piece, (key_part, value_part, piece_offsets))]
    reduce_scatter x1 -> x0, waiting for transfers between devices: 158 us -> none  [per_device(): lax.psum_scatter(lax.map(per_piece, (key_part, value_part, piece_offsets)...]
    dot_general x58 -> x1, matrix products: 146 us -> 0.78 us  [nn(): return jnp.dot(a, b, preferred_element_type=F32)]
    all_gather x2 -> x1, waiting for transfers between devices: 125 us -> 0.01 us  [per_device(): grad_frames = lax.all_gather(grad_out[0], wide, axis=0, tiled=False)]
    psum x1, waiting for transfers between devices: 239 us -> 180 us  [per_device(): conv_total = lax.psum(conv_part, ('z', 'x', 'y'))]
    all_to_all x0 -> x3, blocking collectives: none -> 51.8 us  [the longest x1 43.7 us: per_device(): mine = lax.all_to_all(padded, wide, 0, 0, tiled=True)]
    pallas_call x0 -> x2, Pallas kernels: none -> 46.3 us  [the longest x1 38.8 us: attention(): pl.pallas_call(attention_kernel, grid_spec=pltpu.PrefetchScalarGridSpec(n...]
    lt x32 -> x0, other arithmetic: 44.9 us -> none  [masked_scores(): usable = offset + jnp.arange(key_part.shape[0], dtype=jnp.int32) < length]
  transfers between devices with their start and end apart: 6 -> 12, of which waited for: 6 -> 8; matrix products, arithmetic and copies ran while one was open for 10% -> 10% of each run, Pallas kernels for 0% -> 8%
where the time goes in v1:
time: 464 us; the launch traced here: 463 us
  waiting for transfers between devices  252 us (54%)
  blocking collectives  54.1 us (12%)
  Pallas kernels  46.3 us (10%)
  starting transfers between devices  41.2 us (9%)
  local copies, waits for them, and re-layouts  27.7 us (6%)
  other arithmetic  24.4 us (5%)
  between operations  16.6 us (4%)
    psum x1, waiting for transfers between devices, per_device(): conv_total = lax.psum(conv_part, ('z', 'x', 'y'))  180 us
    all_to_all x1, blocking collectives, per_device(): mine = lax.all_to_all(padded, wide, 0, 0, tiled=True)  43.7 us
    pallas_call x1, Pallas kernels, attention(): pl.pallas_call(attention_kernel, grid_spec=pltpu.PrefetchScalarGridSpec(n...  38.8 us
    ppermute x1, waiting for transfers between devices, with_halo(): right = lax.ppermute(head, axes, [(i + 1, i) for i in range(count - 1)])  34.7 us
    all_to_all x1, waiting for transfers between devices, per_device(): back = lax.all_to_all(back, wide, 0, 0, tiled=True)[:2 * heads]  19.9 us
    all_to_all x2, starting transfers between devices, to_all(): return lax.all_to_all(copies, axes, 0, 0, tiled=True)  11 us
  transfers between devices with their start and end apart: 12, of which 8 were waited for; matrix products, arithmetic and copies ran while one was open for 10% of the time, Pallas kernels for 8%

profile of v1, /device:TPU:4, one launch (start us, length us, event | category | flops | bytes accessed | tf_op | source)
XLA Modules:
  0.0 462.9 jit_solution(645936812821723654)
XLA Ops:
  8.1 0.7 all-gather.3.cloned.1.call-update
  8.7 0.7 convert_element_type.59
  9.6 2.3 all-gather
  11.9 0.8 fusion.1
  13.1 4.4 all_to_all.45
  17.6 43.7 %all_to_all.46.mine.mine_q = bf16[32,128,128]{2,1,0:T(8,128)(2,1)S(1)} all-to-all(bf16[32,128,128]{2,1,0:T(8,128)(2,1)S(1)} %pad.4), channel_id=1, replica_groups=mesh['z'=8,'x'=4,'c'=2,'y'=4] {'x','z'}, dimensions={0} | all-to-all | bytes 2097152 | tf_op jit(solution)/shard_map/all_to_all | solution.py:249
  62.0 2.1 collective-permute-done.other.other_q
  64.0 38.8 %attention.1 = (bf16[2,2560,128]{2,1,0:T(8,128)(2,1)S(1)}, bf16[16,64,128]{2,1,0:T(8,128)(2,1)S(1)}) custom-call(s32[2]{0:T(128)S(1)} %pad_add_fusion.where_ref, bf16[32,128,128]{2,1,0:T(8,128)(2,1)S(1)} %all_to_all.46.mine.mine_q, bf16[32,128,128]{2,1,0:T(8,128)(2,1)} %collective-permute-done.other.other_q, ...), custom_call_target="tpu_custom_call" | custom-call | flops 6442450944 | bytes 4194304 | tf_op jit(solution)/shard_map/attention/pallas_call | solution.py:125
  102.8 1.0 copy-done.1
  103.9 0.7 copy-done.2
  104.6 4.7 %all-to-all-start.2 = ((bf16[2,2560,128]{2,1,0:T(8,128)(2,1)}), bf16[2,2560,128]{2,1,0:T(8,128)(2,1)}, u32[]{:S(2)}, u32[]{:S(2)}) async-start(bf16[2,2560,128]{2,1,0:T(8,128)(2,1)} %copy-done.1), calls=%async_computation.2 | async-start | bytes 2621440 | tf_op jit(solution)/shard_map/all_to_all | solution.py:255
  109.7 1.9 all-to-all-done.2
  111.7 1.0 slice.430
  112.6 1.3 add_convert_fusion
  114.0 1.9 maximum_select_fusion.ctx
  115.9 7.5 %out_weight.1 = f32[64,768]{1,0:T(8,128)} custom-call(bf16[32,64,128]{2,1,0:T(8,128)(2,1)} %maximum_select_fusion.ctx, bf16[32,768,128]{2,1,0:T(8,128)(2,1)} %all-gather.3.cloned.1.call-done.grad), custom_call_target="tpu_custom_call" | custom-call | flops 402653184 | bytes 7340032 | tf_op jit(solution)/shard_map/out_weight/pallas_call | solution.py:169
  123.4 1.6 convert_element_type.65
  125.0 7.7 %all-to-all-start.5 = ((bf16[16,8,384]{2,1,0:T(8,128)(2,1)}), bf16[16,8,384]{2,1,0:T(8,128)(2,1)S(1)}, u32[]{:S(2)}, u32[]{:S(2)}) async-start(bf16[16,8,384]{2,1,0:T(8,128)(2,1)} %bitcast.19), calls=%async_computation.5 | async-start | bytes 196608 | tf_op jit(solution)/shard_map/all_to_all | solution.py:282
  132.7 0.9 pad_maximum_fusion.1
  133.6 4.6 all-to-all-done.5
  138.2 7.9 %all-to-all-start.3 = ((bf16[32,96,128]{2,1,0:T(8,128)(2,1)}), bf16[32,96,128]{2,1,0:T(8,128)(2,1)S(1)}, u32[]{:S(2)}, u32[]{:S(2)}) async-start(bf16[32,96,128]{2,1,0:T(8,128)(2,1)} %pad_maximum_fusion.1), calls=%async_computation.3 | async-start | bytes 1572864 | tf_op jit(solution)/shard_map/all_to_all | solution.py:265
  146.1 19.9 %all-to-all-done.3 = bf16[32,96,128]{2,1,0:T(8,128)(2,1)S(1)} async-done(((bf16[32,96,128]{2,1,0:T(8,128)(2,1)}), bf16[32,96,128]{2,1,0:T(8,128)(2,1)S(1)}, u32[]{:S(2)}, u32[]{:S(2)}) %all-to-all-start.3) | async-done | bytes 786464 | tf_op jit(solution)/shard_map/all_to_all | solution.py:265
  166.0 0.7 broadcast_in_dim.9
  166.7 4.2 all-to-all-start.6
  170.9 0.9 constant_dynamic-update-slice_fusion.1
  171.8 1.0 constant_dynamic-update-slice_fusion
  172.8 0.9 slice.431
  173.6 6.6 %all-to-all-done.6 = bf16[8,3,8,384]{3,2,1,0:T(8,128)(2,1)} async-done(((bf16[8,3,8,384]{3,2,1,0:T(8,128)(2,1)}), bf16[8,3,8,384]{3,2,1,0:T(8,128)(2,1)}, u32[]{:S(2)}, u32[]{:S(2)}) %all-to-all-start.6) | async-done | bytes 147488 | tf_op jit(solution)/shard_map/all_to_all | solution.py:220
  180.2 3.5 all-to-all-start.4
  183.7 0.9 copy.17
  184.7 0.8 all-to-all-done.4
  185.5 3.8 all_to_all.47
  189.3 1.7 broadcast_in_dim.10
  191.1 6.8 %all-to-all-start.8 = ((bf16[16,2,12,8,384]{4,3,2,1,0:T(8,128)(2,1)}), bf16[16,2,12,8,384]{4,3,2,1,0:T(8,128)(2,1)}, u32[]{:S(2)}, u32[]{:S(2)}) async-start(bf16[16,2,12,8,384]{4,3,2,1,0:T(8,128)(2,1)} %broadcast_in_dim.10), calls=%async_computation.8 | async-start | bytes 4718592 | tf_op jit(solution)/shard_map/all_to_all | solution.py:220
  198.1 2.6 collective-permute-start.3
  200.7 3.4 collective-permute-start.2
  204.4 34.7 %collective-permute-done.3 = bf16[2,768,15]{2,1,0:T(8,128)(2,1)S(1)} collective-permute-done((bf16[2,768,15]{2,1,0:T(8,128)(2,1)S(1)}, bf16[2,768,15]{2,1,0:T(8,128)(2,1)S(1)}, u32[]{:S(2)}, u32[]{:S(2)}) %collective-permute-start.3) | collective-permute-done | bytes 46112 | tf_op jit(solution)/shard_map/ppermute | solution.py:193
  239.7 2.6 fusion.14
  242.5 3.7 fusion.32
  246.4 2.6 stack.151
  249.0 7.8 %fusion.67 = bf16[1,768,128]{2,1,0:T(8,128)(2,1)} fusion(f32[768,158]{1,0:T(8,128)S(1)} %get-tuple-element.73, f32[768]{0:T(1024)S(1)} %get-tuple-element.70, f32[768]{0:T(1024)S(1)} %get-tuple-element.71, f32[768]{0:T(1024)S(1)} %get-tuple-element.42, f32[768]{0:T(1024)S(1)} %get-tuple-element.43, f32[768]{0:T(1024)S(1)} %get-tuple-element.44, ...), kind=kLoop, calls=%fused_computation.141 | loop fusion | flops 6094848 | bytes 12481536 | tf_op jit(solution)/shard_map/broadcast_in_dim | solution.py:297
  256.8 0.7 pad_maximum_fusion.3
  257.5 0.8 fusion.68
  258.3 2.3 fusion
  260.7 5.8 %copy.18 = f32[12,8,8,2,2,384]{5,4,3,2,1,0:T(2,128)} copy(f32[12,8,8,2,2,384]{5,2,0,3,4,1:T(8,128)S(1)} %fusion) | data formatting | bytes 9437184 | tf_op jit(solution)/shard_map/mul | solution.py:288
  266.4 7.0 %reshape.100 = f32[768,1536]{1,0:T(8,128)} reshape(f32[12,8,8,2,2,384]{5,4,3,2,1,0:T(2,128)} %copy.18) | data formatting | bytes 9437184 | tf_op jit(solution)/shard_map/reshape | solution.py:288
  273.5 180.4 %all-reduce.3.cloned.1.call-done = f32[31,768]{1,0:T(8,128)} async-done(((f32[31,768]{1,0:T(8,128)}), f32[31,768]{1,0:T(8,128)}) %all-reduce.3.cloned.1.call-update) | async-done | bytes 95248 | tf_op jit(solution)/shard_map/psum | solution.py:291
  453.9 1.5 copy.22
  (74 shorter events, 2.6 us)
Async XLA Ops:
  8.0 3.8 copy-start
  8.0 107.9 %all-gather.3.cloned.1.call-start = ((), (), s32[]{:S(2)}) async-start(), calls=%async_computation.9 | async-start | bytes 6488064 | tf_op jit(solution)/shard_map/all_gather | solution.py:233
  11.8 0.9 copy-start.7
  11.8 1.0 copy-start.8
  11.9 1.1 copy-start.9
  61.3 2.8 collective-permute-start
  102.8 1.1 copy-start.1
  103.9 0.7 copy-start.2
  104.6 4.7 %copy-start.3 = (bf16[16,64,128]{2,1,0:T(8,128)(2,1)S(1)}, bf16[16,64,128]{2,1,0:T(8,128)(2,1)}, u32[]{:S(2)}) copy-start(bf16[16,64,128]{2,1,0:T(8,128)(2,1)} %copy-done.2) | copy-start | bytes 786436
  104.6 7.1 %all-to-all-start.2 = ((bf16[2,2560,128]{2,1,0:T(8,128)(2,1)}), bf16[2,2560,128]{2,1,0:T(8,128)(2,1)}, u32[]{:S(2)}, u32[]{:S(2)}) async-start(bf16[2,2560,128]{2,1,0:T(8,128)(2,1)} %copy-done.1), calls=%async_computation.2 | async-start | bytes 2621440 | tf_op jit(solution)/shard_map/all_to_all | solution.py:255
  109.2 4.7 %collective-permute-start.1 = (bf16[16,64,128]{2,1,0:T(8,128)(2,1)S(1)}, bf16[16,64,128]{2,1,0:T(8,128)(2,1)}, u32[]{:S(2)}, u32[]{:S(2)}) collective-permute-start(bf16[16,64,128]{2,1,0:T(8,128)(2,1)S(1)} %copy-done.3), channel_id=1, source_target_pairs={{0,4},{4,0},{1,5},{5,1},{2,6},{6,2},{3,7},{7,3},{8,12},{12,8},{9,1... | collective-permute-start | bytes 786440 | tf_op jit(solution)/shard_map/ppermute | solution.py:214
  125.0 13.2 %all-to-all-start.5 = ((bf16[16,8,384]{2,1,0:T(8,128)(2,1)}), bf16[16,8,384]{2,1,0:T(8,128)(2,1)S(1)}, u32[]{:S(2)}, u32[]{:S(2)}) async-start(bf16[16,8,384]{2,1,0:T(8,128)(2,1)} %bitcast.19), calls=%async_computation.5 | async-start | bytes 196608 | tf_op jit(solution)/shard_map/all_to_all | solution.py:282
  138.2 27.8 %all-to-all-start.3 = ((bf16[32,96,128]{2,1,0:T(8,128)(2,1)}), bf16[32,96,128]{2,1,0:T(8,128)(2,1)S(1)}, u32[]{:S(2)}, u32[]{:S(2)}) async-start(bf16[32,96,128]{2,1,0:T(8,128)(2,1)} %pad_maximum_fusion.1), calls=%async_computation.3 | async-start | bytes 1572864 | tf_op jit(solution)/shard_map/all_to_all | solution.py:265
  166.7 13.6 %all-to-all-start.6 = ((bf16[8,3,8,384]{3,2,1,0:T(8,128)(2,1)}), bf16[8,3,8,384]{3,2,1,0:T(8,128)(2,1)}, u32[]{:S(2)}, u32[]{:S(2)}) async-start(bf16[8,3,8,384]{3,2,1,0:T(8,128)(2,1)} %broadcast_in_dim.9), calls=%async_computation.6 | async-start | bytes 294912 | tf_op jit(solution)/shard_map/all_to_all | solution.py:220
  180.2 5.3 %all-to-all-start.4 = ((bf16[2,12,96,128]{3,2,1,0:T(8,128)(2,1)}), bf16[2,12,96,128]{3,2,1,0:T(8,128)(2,1)S(1)}, u32[]{:S(2)}, u32[]{:S(2)}) async-start(bf16[2,12,96,128]{3,2,1,0:T(8,128)(2,1)} %bitcast.83), calls=%async_computation.4 | async-start | bytes 1179648 | tf_op jit(solution)/shard_map/all_to_all | solution.py:266
  185.5 5.6 %copy-start.4 = (bf16[2,12,96,128]{3,2,1,0:T(8,128)(2,1)}, bf16[2,12,96,128]{3,2,1,0:T(8,128)(2,1)S(1)}, u32[]{:S(2)}) copy-start(bf16[2,12,96,128]{3,2,1,0:T(8,128)(2,1)S(1)} %all-to-all-done.4) | copy-start | bytes 1769476
  191.1 13.0 %copy-start.10 = (f32[31,768]{1,0:T(8,128)S(1)}, f32[31,768]{1,0:T(8,128)}, u32[]{:S(2)}) copy-start(f32[31,768]{1,0:T(8,128)} %param.19) | copy-start | bytes 285700
  191.1 67.3 %all-to-all-start.8 = ((bf16[16,2,12,8,384]{4,3,2,1,0:T(8,128)(2,1)}), bf16[16,2,12,8,384]{4,3,2,1,0:T(8,128)(2,1)}, u32[]{:S(2)}, u32[]{:S(2)}) async-start(bf16[16,2,12,8,384]{4,3,2,1,0:T(8,128)(2,1)} %broadcast_in_dim.10), calls=%async_computation.8 | async-start | bytes 4718592 | tf_op jit(solution)/shard_map/all_to_all | solution.py:220
  197.9 256.0 %all-reduce.3.cloned.1.call-start = ((), (), s32[]{:S(2)}) async-start(), calls=%async_computation.10 | async-start | bytes 196608 | tf_op jit(solution)/shard_map/psum | solution.py:291
  198.1 41.6 %copy-start.6 = (bf16[1,768,128]{2,1,0:T(8,128)(2,1)S(1)}, bf16[1,768,128]{2,1,0:T(8,128)(2,1)}, u32[]{:S(2)}) copy-start(bf16[1,768,128]{2,1,0:T(8,128)(2,1)} %param.18) | copy-start | bytes 589828
  198.1 40.9 %collective-permute-start.3 = (bf16[2,768,15]{2,1,0:T(8,128)(2,1)S(1)}, bf16[2,768,15]{2,1,0:T(8,128)(2,1)S(1)}, u32[]{:S(2)}, u32[]{:S(2)}) collective-permute-start(bf16[2,768,15]{2,1,0:T(8,128)(2,1)S(1)} %get-tuple-element.79), channel_id=1, source_target_pairs={{8,0},{16,8},{24,16},{32,24},{40,32},{48,40},{56,48},{64,56},{72,6... | collective-permute-start | bytes 138248 | tf_op jit(solution)/shard_map/ppermute | solution.py:193
  200.7 38.4 %collective-permute-start.2 = (bf16[2,768,15]{2,1,0:T(8,128)(2,1)S(1)}, bf16[2,768,15]{2,1,0:T(8,128)(2,1)S(1)}, u32[]{:S(2)}, u32[]{:S(2)}) collective-permute-start(bf16[2,768,15]{2,1,0:T(8,128)(2,1)S(1)} %get-tuple-element.78), channel_id=1, source_target_pairs={{0,8},{8,16},{16,24},{24,32},{32,40},{40,48},{48,56},{56,64},{64,7... | collective-permute-start | bytes 138248 | tf_op jit(solution)/shard_map/ppermute | solution.py:192
  249.0 7.8 %copy-start.5 = (bf16[2,12,96,128]{3,2,1,0:T(8,128)(2,1)S(1)}, bf16[2,12,96,128]{3,2,1,0:T(8,128)(2,1)}, u32[]{:S(2)}) copy-start(bf16[2,12,96,128]{3,2,1,0:T(8,128)(2,1)} %copy-done.4) | copy-start | bytes 1769476
Sparse Core Ops, SparseCore 0:
  11.4 97.5 all-gather.2
Sparse Core Ops, SparseCore 1:
  249.1 204.7 all-reduce.2

commit v2 on v1

--- a/solution.py
+++ b/solution.py
@@ -13,7 +13,7 @@
 BF = jnp.bfloat16
 F32 = jnp.float32
 TWO_SCALE = math.log2(math.e) / 8
-QB = 512
+QB = 1024
 KC = 512
 
 
@@ -26,7 +26,7 @@
 
 
 def attention_kernel(
-    where_ref, mine, other, mine_q, other_q, xch, ctx_out,
+    where_ref, mine, other, mine_q, other_q, kept, sent, ctx_out,
     kt, vt, kn, vn, weights, grad_k, grad_v,
 ):
     blocks, frames = mine.shape[0], mine.shape[2]
@@ -49,8 +49,7 @@
             turned = both.astype(F32)
             kt[here, :DH] = turned[:DH].T.astype(BF)
             vt[here, :DH] = turned[DH:].T.astype(BF)
-            first = ((s % 8) * 4 + s // 8) * frames
-            masked = jnp.logical_and(lane == 0, row + first >= length)
+            masked = jnp.logical_and(lane == 0, row + s * frames >= length)
             kt[here, DH:] = jnp.where(masked, -1e30, 0.0).astype(BF)
             vt[here, DH:] = ones
         vn[DH:, :] = jnp.ones((vn.shape[0] - DH, total), BF)
@@ -102,16 +101,19 @@
         cols = slice(u * frames, (u + 1) * frames)
         ctx_out[u] = context[:, cols]
         at = pl.ds(pl.multiple_of(blocks * DH + (step * sources + u) * half, half), half)
-        xch[0, at, :] = grad_q[:half, cols]
-        xch[1, at, :] = grad_q[half:, cols]
+        low, high_half = grad_q[:half, cols], grad_q[half:, cols]
+        kept[at, :] = jnp.where(core == 0, low, high_half)
+        sent[at, :] = jnp.where(core == 0, high_half, low)
 
     @pl.when(step == pl.num_programs(0) - 1)
     def _():
         for s in range(blocks):
             here = pl.ds(s * frames, frames)
             to = pl.ds(s * DH, DH)
-            xch[0, to, :] = (grad_k[here, :].T * 0.125).astype(BF)
-            xch[1, to, :] = grad_v[here, :].T.astype(BF)
+            of_key = (grad_k[here, :].T * 0.125).astype(BF)
+            of_value = grad_v[here, :].T.astype(BF)
+            kept[to, :] = jnp.where(core == 0, of_key, of_value)
+            sent[to, :] = jnp.where(core == 0, of_value, of_key)
 
 
 def attention(where, mine, other):
@@ -129,7 +131,8 @@
             grid=(steps,),
             in_specs=[whole, whole, part, part],
             out_specs=[
-                pl.BlockSpec((2, blocks * DH + blocks // 2 * (DH // 2), frames), lambda i, w: (0, 0, 0)),
+                pl.BlockSpec((blocks * DH + blocks // 2 * (DH // 2), frames), lambda i, w: (0, 0)),
+                pl.BlockSpec((blocks * DH + blocks // 2 * (DH // 2), frames), lambda i, w: (0, 0)),
                 pl.BlockSpec((sources, DH, frames), lambda i, w: (i, 0, 0)),
             ],
             scratch_shapes=[
@@ -143,7 +146,8 @@
             ],
         ),
         out_shape=[
-            jax.ShapeDtypeStruct((2, blocks * DH + blocks // 2 * (DH // 2), frames), BF),
+            jax.ShapeDtypeStruct((blocks * DH + blocks // 2 * (DH // 2), frames), BF),
+            jax.ShapeDtypeStruct((blocks * DH + blocks // 2 * (DH // 2), frames), BF),
             jax.ShapeDtypeStruct((blocks // 2, DH, frames), BF),
         ],
         compiler_params=pltpu.CompilerParams(
@@ -154,18 +158,31 @@
     )(where, mine, other, mine, other)
 
 
-def out_weight_kernel(ctx, grad, out):
-    @pl.when(pl.program_id(0) == 0)
+def out_weight_kernel(ctx, grad, out, total):
+    step = pl.program_id(0)
+
+    @pl.when(step == 0)
     def _():
-        out[...] = jnp.zeros_like(out)
-
-    for u in range(ctx.shape[0]):
-        out[...] += nt(ctx[u], grad[u])
+        total[...] = jnp.zeros_like(total)
+
+    for u in range(0, ctx.shape[0], 2):
+        total[...] += nt(
+            jnp.concatenate([grad[u], grad[u + 1]], axis=1),
+            jnp.concatenate([ctx[u], ctx[u + 1]], axis=1),
+        )
+
+    @pl.when(step == pl.num_programs(0) - 1)
+    def _():
+        rows = total[...].T.astype(out.dtype)
+        high, wide = out.shape[2], out.shape[3]
+        for q in range(out.shape[0]):
+            for j in range(out.shape[1]):
+                out[q, j] = rows[q * high : (q + 1) * high, j * wide : (j + 1) * wide]
 
 
 def out_weight_part(ctx, grad):
     blocks, channels, frames = grad.shape
-    each = 4
+    each = 8
     return pl.pallas_call(
         out_weight_kernel,
         grid=(blocks // each,),
@@ -173,9 +190,12 @@
             pl.BlockSpec((each, DH, frames), lambda i: (i, 0, 0)),
             pl.BlockSpec((each, channels, frames), lambda i: (i, 0, 0)),
         ],
-        out_specs=pl.BlockSpec((DH, channels), lambda i: (0, 0)),
-        out_shape=jax.ShapeDtypeStruct((DH, channels), F32),
-        compiler_params=pltpu.CompilerParams(dimension_semantics=("arbitrary",)),
+        out_specs=pl.BlockSpec((4, channels // 128, DH // 4, 128), lambda i: (0, 0, 0, 0)),
+        out_shape=jax.ShapeDtypeStruct((4, channels // 128, DH // 4, 128), BF),
+        scratch_shapes=[pltpu.VMEM((channels, DH), F32)],
+        compiler_params=pltpu.CompilerParams(
+            dimension_semantics=("arbitrary",), vmem_limit_bytes=32 * 1024 * 1024
+        ),
         cost_estimate=pl.CostEstimate(
             flops=2 * blocks * DH * channels * frames, bytes_accessed=7 << 20, transcendentals=0
         ),
@@ -183,31 +203,101 @@
     )(ctx, grad)
 
 
-def with_halo(cells, width):
-    frames = cells.shape[2]
-    order = [(z, x) for z in range(8) for x in range(4)]
+def assemble_kernel(core_mask, held, out):
+    core = core_mask[0]
+    x = pl.program_id(0)
+    groups, _, quarters, rows, width = out.shape
+    tiles = width // 2 // 128
+    for g in range(groups):
+        factor = core_mask[1 + g * 4 + x].astype(F32)
+        for q in range(quarters):
+            for side in range(2):
+                first = pl.multiple_of(jnp.where(core == side, 0, width // 2), 128)
+                for j in range(tiles):
+                    at = ((side * groups + g) * tiles + j) * rows
+                    part = held[q, at : at + rows, :].astype(F32) * factor
+                    out[g, 0, q, :, pl.ds(first + j * 128, 128)] = part
+
+
+def assemble(core_mask, held, heads):
+    groups, rows = heads // 4, DH // 4
+    width = 2 * heads * DH
+    out = pl.pallas_call(
+        assemble_kernel,
+        grid_spec=pltpu.PrefetchScalarGridSpec(
+            num_scalar_prefetch=1,
+            grid=(4,),
+            in_specs=[pl.BlockSpec((4, held.shape[1], 128), lambda i, m: (i, 0, 0))],
+            out_specs=pl.BlockSpec((groups, 1, 4, rows, width), lambda i, m: (0, i, 0, 0, 0)),
+        ),
+        out_shape=jax.ShapeDtypeStruct((groups, 4, 4, rows, width), F32),
+        compiler_params=pltpu.CompilerParams(
+            dimension_semantics=("arbitrary",), vmem_limit_bytes=32 * 1024 * 1024
+        ),
+        cost_estimate=pl.CostEstimate(flops=1 << 20, bytes_accessed=7 << 20, transcendentals=0),
+        name="assemble",
+    )(core_mask, held)
+    return out.reshape(heads * DH, width)
+
+
+def halo(array):
     axes = ("z", "x")
-    count = len(order)
-    head, tail = cells[:, :, :width], cells[:, :, frames - width :]
-    left = lax.ppermute(tail, axes, [(i, i + 1) for i in range(count - 1)])
-    right = lax.ppermute(head, axes, [(i + 1, i) for i in range(count - 1)])
-    return jnp.concatenate([left, cells, right], axis=2)
-
-
-def convolution(conv_input, conv_grad, conv_weight):
-    frames = conv_grad.shape[1]
-    half_width = KW // 2
-    rimmed = with_halo(jnp.stack([conv_input, conv_grad]), half_width)
-    input_wide = rimmed[0].astype(F32)
-    grad_wide = rimmed[1].astype(F32)
-    own_grad = conv_grad.astype(F32)
-    grad_input = jnp.zeros(own_grad.shape, F32)
-    tap_sums = []
+    count = lax.axis_size(axes)
+    before = lax.ppermute(array, axes, [(i, i + 1) for i in range(count - 1)])
+    after = lax.ppermute(array, axes, [(i + 1, i) for i in range(count - 1)])
+    return before, after
+
+
+def convolution_kernel(before, own, after, weight, out, sums):
+    rows, frames = own.shape[1], own.shape[2]
+    lane = lax.broadcasted_iota(jnp.int32, (rows, frames), 1)
+    column = lax.broadcasted_iota(jnp.int32, (frames, frames), 1)
+    mine = [own[i].astype(F32) for i in range(2)]
+    rest = [
+        jnp.where(lane >= frames // 2, before[i].astype(F32), after[i].astype(F32))
+        for i in range(2)
+    ]
+
+    def shifted(i, by):
+        if by == 0:
+            return mine[i]
+        inside = pltpu.roll(mine[i], (-by) % frames, 1)
+        outside = pltpu.roll(rest[i], (-by) % frames, 1)
+        here = lane < frames - by if by > 0 else lane >= -by
+        return jnp.where(here, inside, outside)
+
+    total = jnp.zeros((rows, frames), F32)
+    tap_sums = jnp.zeros((rows, frames), F32)
     for tap in range(KW):
-        begin = 2 * half_width - tap
-        grad_input = grad_input + conv_weight[tap][:, None] * grad_wide[:, begin : begin + frames]
-        tap_sums.append(jnp.sum(own_grad * input_wide[:, tap : tap + frames], axis=1))
-    return grad_input.astype(BF), jnp.stack(tap_sums)
+        by = tap - KW // 2
+        total = total + weight[:, tap : tap + 1] * shifted(1, -by)
+        product = mine[1] * shifted(0, by)
+        high = product.astype(BF)
+        low = (product - high.astype(F32)).astype(BF)
+        pick = jnp.where(column == tap, 1.0, 0.0).astype(BF)
+        tap_sums = tap_sums + nn(high, pick) + nn(low, pick)
+    out[...] = total.astype(BF)
+    sums[...] = tap_sums
+
+
+def convolution(before, own, after, weight):
+    _, channels, frames = own.shape
+    rows = 64
+    three = pl.BlockSpec((2, rows, frames), lambda i: (0, i, 0))
+    flat = pl.BlockSpec((rows, frames), lambda i: (i, 0))
+    return pl.pallas_call(
+        convolution_kernel,
+        grid=(channels // rows,),
+        in_specs=[three, three, three, pl.BlockSpec((rows, weight.shape[1]), lambda i: (i, 0))],
+        out_specs=[flat, flat],
+        out_shape=[
+            jax.ShapeDtypeStruct((channels, frames), BF),
+            jax.ShapeDtypeStruct((channels, frames), F32),
+        ],
+        compiler_params=pltpu.CompilerParams(dimension_semantics=("arbitrary",)),
+        cost_estimate=pl.CostEstimate(flops=1 << 30, bytes_accessed=3 << 20, transcendentals=0),
+        name="convolution",
+    )(before, own, after, weight)
 
 
 def swap(array):
@@ -227,10 +317,13 @@
     frames = queries.shape[2]
     width = heads * DH
     core = lax.axis_index("c")
-    wide = ("x", "z")
-    blocks = lax.axis_size(wide)
-
-    grad_frames = lax.all_gather(grad_out[0], wide, axis=0, tiled=False)
+    is_first = core == 0
+    frame_axes = ("z", "x")
+    blocks = lax.axis_size(frame_axes)
+
+    conv_own = jnp.stack([conv_input[0], conv_grad[0]])
+    before, after = halo(conv_own)
+    grad_frames = lax.all_gather(grad_out[0], frame_axes, axis=0, tiled=False)
     grad_full = lax.all_gather(grad_out[0], "c", axis=0, tiled=True)
     mask = jnp.repeat(head_mask.astype(F32), DH)[:, None]
     grad_ctx = (nn(out_weight, grad_full) * mask).astype(BF)
@@ -238,57 +331,90 @@
     def by_head(a):
         return a.reshape(heads, DH, frames)
 
-    first = jnp.stack(
+    key_value = jnp.concatenate([by_head(keys[0]), by_head(values[0])], axis=1)
+    query_grad = jnp.concatenate([by_head(queries[0]), by_head(grad_ctx)], axis=1)
+    theirs = swap(jnp.where(is_first, query_grad, key_value))
+    ours = jnp.where(is_first, key_value, query_grad)
+    padded = jnp.concatenate(
         [
-            jnp.concatenate([by_head(keys[0]), by_head(values[0])], axis=1),
-            jnp.concatenate([by_head(queries[0]), by_head(grad_ctx)], axis=1),
+            jnp.where(is_first, ours, theirs),
+            jnp.where(is_first, theirs, ours),
+            jnp.zeros((blocks - 2 * heads, 2 * DH, frames), BF),
         ]
     )
-    by_core = lax.all_to_all(first, "c", 0, 0, tiled=True).reshape(2 * heads, 2 * DH, frames)
-    padded = jnp.pad(by_core, ((0, blocks - 2 * heads), (0, 0), (0, 0)))
-    mine = lax.all_to_all(padded, wide, 0, 0, tiled=True)
+    padded, before, after = lax.optimization_barrier((padded, before, after))
+    mine = lax.all_to_all(padded, frame_axes, 0, 0, tiled=True)
+    conv_rows = jnp.pad(conv_weight, ((0, 1), (0, 0))).T
+    grad_conv_input, tap_sums = convolution(before, conv_own, after, conv_rows)
+    taps = tap_sums[:, : KW + 1].T.reshape(KW + 1, 4, width // 4)
+    taps = jnp.pad(taps, ((0, 0), (0, 0), (0, 256 - width // 4))).reshape(128, 2, 128)
+    mine, grad_conv_input, taps = lax.optimization_barrier((mine, grad_conv_input, taps))
+    taps = lax.all_to_all(taps, ("z", "x", "y"), 0, 0, tiled=True)
     other = swap(mine)
 
     where = jnp.stack([lengths[0], core.astype(jnp.int32)])
-    xch, ctx = attention(where, mine, other)
-
-    xch = lax.all_to_all(xch, "c", 0, 0, tiled=True)
+    kept, sent, ctx = attention(where, mine, other)
+    kept, sent, ctx, taps = lax.optimization_barrier((kept, sent, ctx, taps))
+
+    got = swap(sent)
+    ctx_other = swap(ctx)
     key_rows = blocks * DH
-    summed = (xch[0, :key_rows].astype(F32) + xch[1, :key_rows].astype(F32)).astype(BF)
-    back = jnp.concatenate(
+    summed = (kept[:key_rows].astype(F32) + got[:key_rows].astype(F32)).astype(BF)
+    dq_ours, dq_theirs = (
+        a[key_rows:].reshape(blocks // 2, DH // 2, frames) for a in (kept, got)
+    )
+    dq = jnp.concatenate(
+        [jnp.where(is_first, dq_ours, dq_theirs), jnp.where(is_first, dq_theirs, dq_ours)]
+    )
+    back = jnp.concatenate([summed.reshape(blocks, DH, frames), dq], axis=1)
+    back = lax.all_to_all(back, frame_axes, 0, 0, tiled=True)
+    ours = lax.dynamic_slice_in_dim(back, core * heads, heads, axis=0)
+    theirs = swap(lax.dynamic_slice_in_dim(back, (1 - core) * heads, heads, axis=0))
+    from_first = jnp.where(is_first, ours, theirs)
+    from_second = jnp.where(is_first, theirs, ours)
+    grad_keys = from_first[:, :DH].reshape(1, width, frames)
+    grad_values = from_second[:, :DH].reshape(1, width, frames)
+    grad_queries = jnp.concatenate([from_first[:, DH:], from_second[:, DH:]], axis=1).reshape(
+        1, width, frames
+    )
+
+    ctx_all = jnp.where(
+        is_first, jnp.concatenate([ctx, ctx_other]), jnp.concatenate([ctx_other, ctx])
+    )
+    part = out_weight_part(ctx_all, grad_frames).reshape(4, -1, 128)
+    y = lax.axis_index("y")
+    held = lax.dynamic_index_in_dim(part, y, keepdims=False).astype(F32)
+    for k in range(1, 4):
+        piece = lax.dynamic_index_in_dim(part, (y + k) % 4, keepdims=False)
+        held = held + lax.ppermute(piece, "y", [(i, (i + k) % 4) for i in range(4)]).astype(F32)
+    tap_row = jnp.sum(taps, axis=0).reshape(-1)[: width // 4]
+    tap_high = tap_row.astype(BF)
+    tap_low = (tap_row - tap_high.astype(F32)).astype(BF)
+    tap_row = jnp.concatenate([tap_high, tap_low]).reshape(-1, 128)
+    tap_count = tap_row.shape[0]
+    held = jnp.concatenate(
+        [held.astype(BF), jnp.pad(tap_row, ((0, 16 - tap_count), (0, 0)))], axis=0
+    )
+    held = to_all(held, "z")
+    part_rows = part.shape[1]
+    groups = heads // 4
+    ours = lax.dynamic_slice_in_dim(held[:, :part_rows], core * groups, groups, axis=0)
+    theirs = swap(lax.dynamic_slice_in_dim(held[:, :part_rows], (1 - core) * groups, groups, axis=0))
+    tap_rows = held[:, part_rows : part_rows + tap_count].reshape(-1, 128)
+    spread = jnp.concatenate(
         [
-            summed.reshape(blocks, DH, frames),
-            xch[:, key_rows:].reshape(blocks, DH // 2, frames),
-        ],
-        axis=1,
-    )
-    back = lax.all_to_all(back, wide, 0, 0, tiled=True)[: 2 * heads]
-    back = lax.all_to_all(
-        back.reshape(2, heads, DH + DH // 2, frames), "c", 0, 0, tiled=True
-    )
-    grad_keys = back[0, :, :DH].reshape(1, width, frames)
-    grad_values = back[1, :, :DH].reshape(1, width, frames)
-    grad_queries = jnp.concatenate([back[0, :, DH:], back[1, :, DH:]], axis=1).reshape(
-        1, width, frames
-    )
-
-    ctx_other = swap(ctx)
-    ctx_all = jnp.where(
-        core == 0, jnp.concatenate([ctx, ctx_other]), jnp.concatenate([ctx_other, ctx])
-    )
-    part = out_weight_part(ctx_all, grad_frames).astype(BF)
-    cols = width // 2
-    pieces = part.reshape(8, 8, 2, cols).transpose(0, 2, 1, 3).reshape(16, 8, cols)
-    pieces = lax.all_to_all(pieces, ("x", "y"), 0, 0, tiled=True).reshape(4, 4, 8, cols)
-    held = jnp.sum(pieces[:3].astype(F32), axis=1).astype(BF)
-    held = to_all(held, "z").transpose(1, 0, 2, 3).reshape(2, heads, 8, cols)
-    held = lax.all_to_all(held, "c", 0, 0, tiled=True)
-    held = to_all(held, ("x", "y")).reshape(8, 2, 2, heads, 8, cols)
-    own_mask = head_mask.astype(F32)[:, None, None, None, None, None]
-    grad_out_weight = (held.transpose(3, 0, 4, 2, 1, 5).astype(F32) * own_mask).reshape(width, 2 * width)
-
-    grad_conv_input, conv_part = convolution(conv_input[0], conv_grad[0], conv_weight)
-    conv_total = lax.psum(conv_part, ("z", "x", "y"))
+            ours.reshape(-1, 128),
+            theirs.reshape(-1, 128),
+            jnp.pad(tap_rows, ((0, -tap_rows.shape[0] % 16), (0, 0))),
+        ]
+    )
+    held = to_all(spread, ("x", "y"))
+    core_mask = jnp.concatenate([where[1:], head_mask])
+    grad_out_weight = assemble(core_mask, held, heads)
+    first = 2 * groups * part_rows
+    tap_rows = held[:, first : first + tap_rows.shape[0]].astype(F32)
+    tap_rows = tap_rows.reshape(16, 8, 2, width // 4).sum(axis=2).transpose(1, 0, 2)
+    conv_total = tap_rows.reshape(KW + 1, width)[:KW]
     return (
         grad_queries,
         grad_keys,

time: 464 us -> 232 us (0.50)
  waiting for transfers between devices: 252 us -> 71.4 us
  blocking collectives: 54.1 us -> 2.29 us
  other arithmetic: 24.4 us -> 10.5 us
  starting transfers between devices: 41.2 us -> 55.1 us
  Pallas kernels: 46.3 us -> 56.6 us
  local copies, waits for them, and re-layouts: 27.7 us -> 17.8 us
    psum x1 -> x0, waiting for transfers between devices: 180 us -> none  [per_device(): conv_total = lax.psum(conv_part, ('z', 'x', 'y'))]
    all_to_all x3 -> x0, blocking collectives: 51.8 us -> none  [the longest x1 43.7 us: per_device(): mine = lax.all_to_all(padded, wide, 0, 0, tiled=True)]
    all_to_all x2, waiting for transfers between devices: 6.61 us -> 30.7 us  [to_all(): return lax.all_to_all(copies, axes, 0, 0, tiled=True)]
    ppermute x2 -> x5, waiting for transfers between devices: 34.7 us -> 13 us  [the longest x1 5.97 us: halo(): before = lax.ppermute(array, axes, [(i, i + 1) for i in range(count - 1)])]
    pallas_call x0 -> x2, Pallas kernels: none -> 20.9 us  [the longest x1 16 us: convolution(): pl.pallas_call(convolution_kernel, grid=(channels // rows,), in_specs=[th...]
    broadcast_in_dim x1 -> x0, other arithmetic: 7.78 us -> none  [per_device(): grad_conv_input[None]]
    all_to_all x4 -> x3, starting transfers between devices: 23.7 us -> 30.6 us  [the longest x1 15.5 us: per_device(): mine = lax.all_to_all(padded, frame_axes, 0, 0, tiled=True)]
    pallas_call x1, Pallas kernels: 38.8 us -> 32.7 us  [attention(): pl.pallas_call(attention_kernel, grid_spec=pltpu.PrefetchScalarGridSpec(n...]
  transfers between devices with their start and end apart: 12 -> 17, of which waited for: 8 -> 11; matrix products, arithmetic and copies ran while one was open for 10% -> 8% of each run, Pallas kernels for 8% -> 22%
where the time goes in v2:
time: 232 us; the launch traced here: 230 us
  waiting for transfers between devices  71.4 us (31%)
  Pallas kernels  56.6 us (24%)
  starting transfers between devices  55.1 us (24%)
  local copies, waits for them, and re-layouts  17.8 us (8%)
  between operations  15 us (6%)
  other arithmetic  10.5 us (5%)
    pallas_call x1, Pallas kernels, attention(): pl.pallas_call(attention_kernel, grid_spec=pltpu.PrefetchScalarGridSpec(n...  32.7 us
    all_to_all x2, waiting for transfers between devices, to_all(): return lax.all_to_all(copies, axes, 0, 0, tiled=True)  30.7 us
    all_to_all x1, waiting for transfers between devices, per_device(): back = lax.all_to_all(back, frame_axes, 0, 0, tiled=True)  17.5 us
    pallas_call x1, Pallas kernels, convolution(): pl.pallas_call(convolution_kernel, grid=(channels // rows,), in_specs=[th...  16 us
    all_to_all x1, starting transfers between devices, per_device(): mine = lax.all_to_all(padded, frame_axes, 0, 0, tiled=True)  15.5 us
    all_to_all x2, starting transfers between devices, to_all(): return lax.all_to_all(copies, axes, 0, 0, tiled=True)  13.2 us
    all_to_all x1, starting transfers between devices, per_device(): taps = lax.all_to_all(taps, ('z', 'x', 'y'), 0, 0, tiled=True)  10.1 us
    unnamed x32, local copies, waits for them, and re-layouts  7.28 us
  transfers between devices with their start and end apart: 17, of which 11 were waited for; matrix products, arithmetic and copies ran while one was open for 8% of the time, Pallas kernels for 22%

profile of v2, /device:TPU:4, one launch (start us, length us, event | category | flops | bytes accessed | tf_op | source)
XLA Modules:
  0.0 229.6 jit_solution(12637761811634943208)
XLA Ops:
  8.7 2.3 all-gather
  11.1 0.8 fusion
  12.6 3.1 %collective-permute-start.1 = (bf16[2,768,128]{2,1,0:T(8,128)(2,1)S(1)}, bf16[2,768,128]{2,1,0:T(8,128)(2,1)S(1)}, u32[]{:S(2)}, u32[]{:S(2)}) collective-permute-start(bf16[2,768,128]{2,1,0:T(8,128)(2,1)S(1)} %constant_dynamic-update-slice_fusion.own), channel_id=1, source_target_pairs={{0,8},{8,16},{16,24},{24,32},{32,40},{40,48},{48,56},{56,64},{64,7... | collective-permute-start | bytes 1179656 | tf_op jit(solution)/shard_map/ppermute | solution.py:246
  15.7 2.7 %collective-permute-start.2 = (bf16[2,768,128]{2,1,0:T(8,128)(2,1)S(1)}, bf16[2,768,128]{2,1,0:T(8,128)(2,1)}, u32[]{:S(2)}, u32[]{:S(2)}) collective-permute-start(bf16[2,768,128]{2,1,0:T(8,128)(2,1)S(1)} %constant_dynamic-update-slice_fusion.own), channel_id=1, source_target_pairs={{8,0},{16,8},{24,16},{32,24},{40,32},{48,40},{56,48},{64,56},{72,6... | collective-permute-start | bytes 1179656 | tf_op jit(solution)/shard_map/ppermute | solution.py:247
  18.7 1.1 maximum_maximum_fusion
  19.9 6.0 %collective-permute-done.1.before = bf16[2,768,128]{2,1,0:T(8,128)(2,1)S(1)} collective-permute-done((bf16[2,768,128]{2,1,0:T(8,128)(2,1)S(1)}, bf16[2,768,128]{2,1,0:T(8,128)(2,1)S(1)}, u32[]{:S(2)}, u32[]{:S(2)}) %collective-permute-start.1) | collective-permute-done | bytes 393248 | tf_op jit(solution)/shard_map/ppermute | solution.py:246
  25.8 0.8 copy-done.13
  26.6 2.9 %collective-permute-done.2.after = bf16[2,768,128]{2,1,0:T(8,128)(2,1)} collective-permute-done((bf16[2,768,128]{2,1,0:T(8,128)(2,1)S(1)}, bf16[2,768,128]{2,1,0:T(8,128)(2,1)}, u32[]{:S(2)}, u32[]{:S(2)}) %collective-permute-start.2) | collective-permute-done | bytes 393248 | tf_op jit(solution)/shard_map/ppermute | solution.py:247
  29.6 15.5 %all-to-all-start = ((bf16[32,128,128]{2,1,0:T(8,128)(2,1)}), bf16[32,128,128]{2,1,0:T(8,128)(2,1)S(1)}, u32[]{:S(2)}, u32[]{:S(2)}) async-start(bf16[32,128,128]{2,1,0:T(8,128)(2,1)} %maximum_maximum_fusion), calls=%async_computation | async-start | bytes 2097152 | tf_op jit(solution)/shard_map/all_to_all | solution.py:346
  45.1 1.0 copy.21
  46.1 1.8 pad_bitcast_fusion.weight
  47.9 16.0 %convolution.5 = (bf16[768,128]{1,0:T(8,128)(2,1)}, f32[768,128]{1,0:T(8,128)}) custom-call(bf16[2,768,128]{2,1,0:T(8,128)(2,1)} %copy-done.13, bf16[2,768,128]{2,1,0:T(8,128)(2,1)} %copy-done.11, bf16[2,768,128]{2,1,0:T(8,128)(2,1)} %collective-permute-done.2.after, f32[768,32]{1,0:T(8,128)} %pad_bitcast_fusion.weight), custom_call_target="tpu_custom_call" | custom-call | flops 1073741824 | bytes 3145728 | tf_op jit(solution)/shard_map/convolution/pallas_call | solution.py:288
  63.9 1.8 copy.22
  65.7 0.9 pad.17
  66.6 0.8 reshape.76
  67.4 5.2 %all-to-all-done.mine.mine_q = bf16[32,128,128]{2,1,0:T(8,128)(2,1)S(1)} async-done(((bf16[32,128,128]{2,1,0:T(8,128)(2,1)}), bf16[32,128,128]{2,1,0:T(8,128)(2,1)S(1)}, u32[]{:S(2)}, u32[]{:S(2)}) %all-to-all-start) | async-done | bytes 1048608 | tf_op jit(solution)/shard_map/all_to_all | solution.py:346
  73.3 10.1 %all-to-all-start.1 = ((f32[128,2,128]{2,1,0:T(2,128)}), f32[128,2,128]{2,1,0:T(2,128)S(1)}, u32[]{:S(2)}, u32[]{:S(2)}) async-start(f32[128,2,128]{2,1,0:T(2,128)} %reshape.76), calls=%async_computation.1 | async-start | bytes 262144 | tf_op jit(solution)/shard_map/all_to_all | solution.py:352
  83.4 32.7 %attention.1 = (bf16[2560,128]{1,0:T(8,128)(2,1)S(1)}, bf16[2560,128]{1,0:T(8,128)(2,1)S(1)}, bf16[16,64,128]{2,1,0:T(8,128)(2,1)S(1)}) custom-call(s32[2]{0:T(128)S(1)} %pad_add_fusion.where_ref, bf16[32,128,128]{2,1,0:T(8,128)(2,1)S(1)} %all-to-all-done.mine.mine_q, bf16[32,128,128]{2,1,0:T(8,128)(2,1)} %collective-permute-done.3.other.other_q, ...), custom_call_target="tpu_custom_call" | custom-call | flops 6442450944 | bytes 4194304 | tf_op jit(solution)/shard_map/attention/pallas_call | solution.py:127
  116.1 0.8 copy-done.2
  117.0 0.7 copy-done.4
  117.7 0.8 copy-done.5
  119.2 1.4 collective-permute-done.6
  120.6 1.2 maximum_select_fusion.ctx
  121.8 2.8 %copy-done.1 = bf16[32,768,128]{2,1,0:T(8,128)(2,1)S(1)} copy-done((bf16[32,768,128]{2,1,0:T(8,128)(2,1)S(1)}, bf16[32,768,128]{2,1,0:T(8,128)(2,1)}, u32[]{:S(2)}) %copy-start.1) | copy-done | bytes 6291480
  124.6 3.0 %out_weight.1 = bf16[4,6,16,128]{3,2,1,0:T(8,128)(2,1)S(1)} custom-call(bf16[32,64,128]{2,1,0:T(8,128)(2,1)S(1)} %maximum_select_fusion.ctx, bf16[32,768,128]{2,1,0:T(8,128)(2,1)S(1)} %copy-done.1), custom_call_target="tpu_custom_call" | custom-call | flops 402653184 | bytes 7340032 | tf_op jit(solution)/shard_map/out_weight/pallas_call | solution.py:186
  127.6 2.7 %collective-permute-start.9 = (bf16[96,128]{1,0:T(8,128)(2,1)S(1)}, bf16[96,128]{1,0:T(8,128)(2,1)S(1)}, u32[]{:S(2)}, u32[]{:S(2)}) collective-permute-start(bf16[96,128]{1,0:T(8,128)(2,1)S(1)} %get-tuple-element.47), channel_id=1, source_target_pairs={{0,3},{1,0},{2,1},{3,2},{4,7},{5,4},{6,5},{7,6},{8,11},{9,8},{10,9... | collective-permute-start | bytes 73736 | tf_op jit(solution)/shard_map/ppermute | solution.py:389
  130.4 0.9 collective-permute-start.8
  131.2 0.9 collective-permute-start.7
  132.2 3.5 %collective-permute-done.8 = bf16[96,128]{1,0:T(8,128)(2,1)S(1)} collective-permute-done((bf16[96,128]{1,0:T(8,128)(2,1)S(1)}, bf16[96,128]{1,0:T(8,128)(2,1)S(1)}, u32[]{:S(2)}, u32[]{:S(2)}) %collective-permute-start.8) | collective-permute-done | bytes 24608 | tf_op jit(solution)/shard_map/ppermute | solution.py:389
  136.3 0.7 broadcast_in_dim.23
  137.0 7.0 %all-to-all-start.3 = ((bf16[8,112,128]{2,1,0:T(8,128)(2,1)}), bf16[8,112,128]{2,1,0:T(8,128)(2,1)S(1)}, u32[]{:S(2)}, u32[]{:S(2)}) async-start(bf16[8,112,128]{2,1,0:T(8,128)(2,1)} %broadcast_in_dim.23), calls=%async_computation.3 | async-start | bytes 458752 | tf_op jit(solution)/shard_map/all_to_all | solution.py:310
  144.1 1.2 add_convert_fusion
  145.2 0.9 broadcast_select_fusion.7
  146.2 0.9 maximum_maximum_fusion.1
  147.1 7.1 %all-to-all-done.3 = bf16[8,112,128]{2,1,0:T(8,128)(2,1)S(1)} async-done(((bf16[8,112,128]{2,1,0:T(8,128)(2,1)}), bf16[8,112,128]{2,1,0:T(8,128)(2,1)S(1)}, u32[]{:S(2)}, u32[]{:S(2)}) %all-to-all-start.3) | async-done | bytes 229408 | tf_op jit(solution)/shard_map/all_to_all | solution.py:310
  154.2 5.0 %all-to-all-start.2 = ((bf16[32,96,128]{2,1,0:T(8,128)(2,1)}), bf16[32,96,128]{2,1,0:T(8,128)(2,1)S(1)}, u32[]{:S(2)}, u32[]{:S(2)}) async-start(bf16[32,96,128]{2,1,0:T(8,128)(2,1)} %maximum_maximum_fusion.1), calls=%async_computation.2 | async-start | bytes 1572864 | tf_op jit(solution)/shard_map/all_to_all | solution.py:370
  159.3 1.4 collective-permute-done.10
  160.7 0.9 fusion.3
  161.6 17.5 %all-to-all-done.2 = bf16[32,96,128]{2,1,0:T(8,128)(2,1)S(1)} async-done(((bf16[32,96,128]{2,1,0:T(8,128)(2,1)}), bf16[32,96,128]{2,1,0:T(8,128)(2,1)S(1)}, u32[]{:S(2)}, u32[]{:S(2)}) %all-to-all-start.2) | async-done | bytes 786464 | tf_op jit(solution)/shard_map/all_to_all | solution.py:370
  179.1 1.8 broadcast_in_dim.24
  180.8 6.2 %all-to-all-start.4 = ((bf16[16,608,128]{2,1,0:T(8,128)(2,1)}), bf16[16,608,128]{2,1,0:T(8,128)(2,1)}, u32[]{:S(2)}, u32[]{:S(2)}) async-start(bf16[16,608,128]{2,1,0:T(8,128)(2,1)} %broadcast_in_dim.24), calls=%async_computation.4 | async-start | bytes 4980736 | tf_op jit(solution)/shard_map/all_to_all | solution.py:310
  187.2 1.6 collective-permute-done.5
  188.8 1.0 broadcast_select_fusion.5
  189.8 0.7 slice.61
  191.9 23.6 %all-to-all-done.4.held = bf16[16,608,128]{2,1,0:T(8,128)(2,1)} async-done(((bf16[16,608,128]{2,1,0:T(8,128)(2,1)}), bf16[16,608,128]{2,1,0:T(8,128)(2,1)}, u32[]{:S(2)}, u32[]{:S(2)}) %all-to-all-start.4) | async-done | bytes 2490400 | tf_op jit(solution)/shard_map/all_to_all | solution.py:310
  215.5 0.9 slice_convert_fusion
  217.0 0.7 reshape.90
  217.8 4.9 %assemble.1 = f32[3,4,4,16,1536]{4,3,2,1,0:T(8,128)} custom-call(s32[13]{0:T(128)S(1)} %pad_add_fusion.1.core_mask, bf16[16,608,128]{2,1,0:T(8,128)(2,1)} %all-to-all-done.4.held), custom_call_target="tpu_custom_call" | custom-call | flops 1048576 | bytes 7340032 | tf_op jit(solution)/shard_map/assemble/pallas_call | solution.py:225
  (69 shorter events, 6.3 us)
Async XLA Ops:
  7.2 3.9 %copy-start = (bf16[768,1536]{1,0:T(8,128)(2,1)S(1)}, bf16[768,1536]{1,0:T(8,128)(2,1)}, u32[]{:S(2)}) copy-start(bf16[768,1536]{1,0:T(8,128)(2,1)} %param.14) | copy-start | bytes 7077892
  7.2 114.7 %all-gather.3.cloned.1.call-start = ((), (), s32[]{:S(2)}) async-start(), calls=%async_computation.5 | async-start | bytes 6488064 | tf_op jit(solution)/shard_map/all_gather | solution.py:326
  11.0 0.9 copy-start.6
  11.0 1.0 copy-start.7
  11.0 1.1 copy-start.8
  11.0 1.4 copy-start.9
  11.0 1.5 copy-start.10
  12.3 6.3 %collective-permute-start = (bf16[12,128,128]{2,1,0:T(8,128)(2,1)S(1)}, bf16[12,128,128]{2,1,0:T(8,128)(2,1)S(1)}, u32[]{:S(2)}, u32[]{:S(2)}) collective-permute-start(bf16[12,128,128]{2,1,0:T(8,128)(2,1)S(1)} %broadcast_select_fusion.2), channel_id=1, source_target_pairs={{0,4},{4,0},{1,5},{5,1},{2,6},{6,2},{3,7},{7,3},{8,12},{12,8},{9,1... | collective-permute-start | bytes 1179656 | tf_op jit(solution)/shard_map/ppermute | solution.py:304
  12.5 7.3 %copy-start.11 = (bf16[2,768,128]{2,1,0:T(8,128)(2,1)}, bf16[2,768,128]{2,1,0:T(8,128)(2,1)S(1)}, u32[]{:S(2)}) copy-start(bf16[2,768,128]{2,1,0:T(8,128)(2,1)S(1)} %constant_dynamic-update-slice_fusion.own) | copy-start | bytes 1179652
  12.6 13.3 %collective-permute-start.1 = (bf16[2,768,128]{2,1,0:T(8,128)(2,1)S(1)}, bf16[2,768,128]{2,1,0:T(8,128)(2,1)S(1)}, u32[]{:S(2)}, u32[]{:S(2)}) collective-permute-start(bf16[2,768,128]{2,1,0:T(8,128)(2,1)S(1)} %constant_dynamic-update-slice_fusion.own), channel_id=1, source_target_pairs={{0,8},{8,16},{16,24},{24,32},{32,40},{40,48},{48,56},{56,64},{64,7... | collective-permute-start | bytes 1179656 | tf_op jit(solution)/shard_map/ppermute | solution.py:246
  15.7 13.9 %collective-permute-start.2 = (bf16[2,768,128]{2,1,0:T(8,128)(2,1)S(1)}, bf16[2,768,128]{2,1,0:T(8,128)(2,1)}, u32[]{:S(2)}, u32[]{:S(2)}) collective-permute-start(bf16[2,768,128]{2,1,0:T(8,128)(2,1)S(1)} %constant_dynamic-update-slice_fusion.own), channel_id=1, source_target_pairs={{8,0},{16,8},{24,16},{32,24},{40,32},{48,40},{56,48},{64,56},{72,6... | collective-permute-start | bytes 1179656 | tf_op jit(solution)/shard_map/ppermute | solution.py:247
  18.7 26.3 %copy-start.12 = (f32[31,768]{1,0:T(8,128)S(1)}, f32[31,768]{1,0:T(8,128)}, u32[]{:S(2)}) copy-start(f32[31,768]{1,0:T(8,128)} %param.19) | copy-start | bytes 285700
  25.8 0.8 copy-start.13
  29.6 43.0 %all-to-all-start = ((bf16[32,128,128]{2,1,0:T(8,128)(2,1)}), bf16[32,128,128]{2,1,0:T(8,128)(2,1)S(1)}, u32[]{:S(2)}, u32[]{:S(2)}) async-start(bf16[32,128,128]{2,1,0:T(8,128)(2,1)} %maximum_maximum_fusion), calls=%async_computation | async-start | bytes 2097152 | tf_op jit(solution)/shard_map/all_to_all | solution.py:346
  72.5 10.9 %collective-permute-start.3 = (bf16[32,128,128]{2,1,0:T(8,128)(2,1)S(1)}, bf16[32,128,128]{2,1,0:T(8,128)(2,1)}, u32[]{:S(2)}, u32[]{:S(2)}) collective-permute-start(bf16[32,128,128]{2,1,0:T(8,128)(2,1)S(1)} %all-to-all-done.mine.mine_q), channel_id=1, source_target_pairs={{0,4},{4,0},{1,5},{5,1},{2,6},{6,2},{3,7},{7,3},{8,12},{12,8},{9,1... | collective-permute-start | bytes 3145736 | tf_op jit(solution)/shard_map/ppermute | solution.py:304
  73.3 45.3 %all-to-all-start.1 = ((f32[128,2,128]{2,1,0:T(2,128)}), f32[128,2,128]{2,1,0:T(2,128)S(1)}, u32[]{:S(2)}, u32[]{:S(2)}) async-start(f32[128,2,128]{2,1,0:T(2,128)} %reshape.76), calls=%async_computation.1 | async-start | bytes 262144 | tf_op jit(solution)/shard_map/all_to_all | solution.py:352
  116.1 0.8 copy-start.2
  117.0 0.7 copy-start.4
  117.7 0.8 copy-start.5
  118.6 2.1 collective-permute-start.6
  118.6 25.5 %collective-permute-start.4 = (bf16[2560,128]{1,0:T(8,128)(2,1)}, bf16[2560,128]{1,0:T(8,128)(2,1)}, u32[]{:S(2)}, u32[]{:S(2)}) collective-permute-start(bf16[2560,128]{1,0:T(8,128)(2,1)} %copy-done.5), channel_id=1, source_target_pairs={{0,4},{4,0},{1,5},{5,1},{2,6},{6,2},{3,7},{7,3},{8,12},{12,8},{9,1... | collective-permute-start | bytes 1966088 | tf_op jit(solution)/shard_map/ppermute | solution.py:304
  121.8 2.8 %copy-start.1 = (bf16[32,768,128]{2,1,0:T(8,128)(2,1)S(1)}, bf16[32,768,128]{2,1,0:T(8,128)(2,1)}, u32[]{:S(2)}) copy-start(bf16[32,768,128]{2,1,0:T(8,128)(2,1)} %all-gather.3.cloned.1.call-done.grad) | copy-start | bytes 18874372
  124.6 19.4 %copy-start.3 = (bf16[2560,128]{1,0:T(8,128)(2,1)S(1)}, bf16[2560,128]{1,0:T(8,128)(2,1)}, u32[]{:S(2)}) copy-start(bf16[2560,128]{1,0:T(8,128)(2,1)} %copy-done.2) | copy-start | bytes 1966084
  127.6 4.5 %collective-permute-start.9 = (bf16[96,128]{1,0:T(8,128)(2,1)S(1)}, bf16[96,128]{1,0:T(8,128)(2,1)S(1)}, u32[]{:S(2)}, u32[]{:S(2)}) collective-permute-start(bf16[96,128]{1,0:T(8,128)(2,1)S(1)} %get-tuple-element.47), channel_id=1, source_target_pairs={{0,3},{1,0},{2,1},{3,2},{4,7},{5,4},{6,5},{7,6},{8,11},{9,8},{10,9... | collective-permute-start | bytes 73736 | tf_op jit(solution)/shard_map/ppermute | solution.py:389
  130.4 5.3 %collective-permute-start.8 = (bf16[96,128]{1,0:T(8,128)(2,1)S(1)}, bf16[96,128]{1,0:T(8,128)(2,1)S(1)}, u32[]{:S(2)}, u32[]{:S(2)}) collective-permute-start(bf16[96,128]{1,0:T(8,128)(2,1)S(1)} %get-tuple-element.48), channel_id=1, source_target_pairs={{0,2},{1,3},{2,0},{3,1},{4,6},{5,7},{6,4},{7,5},{8,10},{9,11},{10,... | collective-permute-start | bytes 73736 | tf_op jit(solution)/shard_map/ppermute | solution.py:389
  131.2 5.0 %collective-permute-start.7 = (bf16[96,128]{1,0:T(8,128)(2,1)S(1)}, bf16[96,128]{1,0:T(8,128)(2,1)S(1)}, u32[]{:S(2)}, u32[]{:S(2)}) collective-permute-start(bf16[96,128]{1,0:T(8,128)(2,1)S(1)} %get-tuple-element.46), channel_id=1, source_target_pairs={{0,1},{1,2},{2,3},{3,0},{4,5},{5,6},{6,7},{7,4},{8,9},{9,10},{10,1... | collective-permute-start | bytes 73736 | tf_op jit(solution)/shard_map/ppermute | solution.py:389
  137.0 17.2 %all-to-all-start.3 = ((bf16[8,112,128]{2,1,0:T(8,128)(2,1)}), bf16[8,112,128]{2,1,0:T(8,128)(2,1)S(1)}, u32[]{:S(2)}, u32[]{:S(2)}) async-start(bf16[8,112,128]{2,1,0:T(8,128)(2,1)} %broadcast_in_dim.23), calls=%async_computation.3 | async-start | bytes 458752 | tf_op jit(solution)/shard_map/all_to_all | solution.py:310
  154.2 24.9 %all-to-all-start.2 = ((bf16[32,96,128]{2,1,0:T(8,128)(2,1)}), bf16[32,96,128]{2,1,0:T(8,128)(2,1)S(1)}, u32[]{:S(2)}, u32[]{:S(2)}) async-start(bf16[32,96,128]{2,1,0:T(8,128)(2,1)} %maximum_maximum_fusion.1), calls=%async_computation.2 | async-start | bytes 1572864 | tf_op jit(solution)/shard_map/all_to_all | solution.py:370
  159.2 1.5 collective-permute-start.10
  180.8 6.3 %copy-start.14 = (s32[12]{0:T(128)S(1)}, s32[12]{0:T(128)}, u32[]{:S(2)}) copy-start(s32[12]{0:T(128)} %param.15) | copy-start | bytes 148
  180.8 34.7 %all-to-all-start.4 = ((bf16[16,608,128]{2,1,0:T(8,128)(2,1)}), bf16[16,608,128]{2,1,0:T(8,128)(2,1)}, u32[]{:S(2)}, u32[]{:S(2)}) async-start(bf16[16,608,128]{2,1,0:T(8,128)(2,1)} %broadcast_in_dim.24), calls=%async_computation.4 | async-start | bytes 4980736 | tf_op jit(solution)/shard_map/all_to_all | solution.py:310
  187.0 1.8 collective-permute-start.5
Sparse Core Ops, SparseCore 0:
  10.6 97.0 all-gather.2
